TPU v7x, 128 devices: a whole 4x4x4 slice. The times are simulated.
128 devices in a mesh: section: 2 (over z_lo), dp: 8 (over x, core), tensor: 8 (over y, z_hi).
Axes of the slice: x: 4, y: 4, z: 4 (z_hi: 2, z_lo: 2; z = z_hi * 2 + z_lo), core: 2. Of those that a mesh axis runs over, the one named last changes fastest.
Arguments:
- tokens: bfloat16 [256, 12288], P('tensor', 'dp'), may hold values from -6 to 6
- out_grad: bfloat16 [256, 12288], P('tensor', 'dp'), may hold values from -6 to 6
- norm_gain: float32 [2, 12288], P('section'), may hold values from 0.1 to 1.9
- norm_shift: float32 [2, 12288], P('section'), may hold values from -3 to 3
- up_weight: bfloat16 [2, 12288, 24576], P('section', 'dp', 'tensor'), may hold values from -0.0546875 to 0.0546875
- up_bias: float32 [2, 24576], P('section'), may hold values from -3 to 3
- down_weight: bfloat16 [2, 24576, 12288], P('section', 'tensor', 'dp'), may hold values from -0.0390625 to 0.0390625
- down_bias: float32 [2, 12288], P('section'), may hold values from -3 to 3
Outputs:
- segment_output: bfloat16 [2, 256, 12288], P('section', 'tensor', 'dp')
- segment_input_grad: bfloat16 [2, 256, 12288], P('section', 'tensor', 'dp')
All inputs are finite; a program needn't handle non-finite values.
Results may differ from a plain program's by a relative error of at most 0.0095.
Values may be sent and summed in bfloat16 or wider, within the bound.
A program may use at most 128 MiB of HBM per device.

v0:
```python
import jax
import jax.numpy as jnp
from jax import lax
from jax.sharding import PartitionSpec as P

D = 12288


epsilon = 1e-05
root_scale = 0.7978845608028654
cubic_term = 0.044715


def passed_along(value, axis, steps):
    count = lax.axis_size(axis)
    leading, last = (max(0, -steps), min(count, count - steps))
    return lax.ppermute(value, axis, [(source, source + steps) for source in range(leading, last)])


def gelu_value(pre_act):
    inner = root_scale * (pre_act + cubic_term * pre_act * pre_act * pre_act)
    return 0.5 * pre_act * (1.0 + jnp.tanh(inner))


def gelu_slope(pre_act):
    inner = root_scale * (pre_act + cubic_term * pre_act * pre_act * pre_act)
    tangent = jnp.tanh(inner)
    return 0.5 * (1.0 + tangent) + 0.5 * pre_act * (1.0 - tangent * tangent) * root_scale * (
        1.0 + 3.0 * cubic_term * pre_act * pre_act
    )


def feature_total(values, first):
    if first:
        return lax.psum(values, "dp")
    return lax.psum(values, "tensor")


def multiply_rows(matrix, transposed, row_block):
    if transposed:
        return lax.dot_general(
            row_block, matrix, (((1,), (1,)), ((), ())), preferred_element_type=jnp.float32
        )
    return jnp.dot(row_block, matrix, preferred_element_type=jnp.float32)


def to_hidden(row_block, matrix, transposed, first):
    if first:
        gathered = lax.all_gather(row_block, "tensor", axis=0, tiled=True)
    else:
        gathered = lax.all_gather(row_block, "dp", axis=0, tiled=True)

    def hidden_term():
        return multiply_rows(matrix, transposed, gathered)

    if first:
        return lax.psum_scatter(hidden_term(), "dp", scatter_dimension=0, tiled=True)
    return lax.psum_scatter(hidden_term(), "tensor", scatter_dimension=0, tiled=True)


def to_model(hidden_block, matrix, transposed, first):
    if first:
        gathered = lax.all_gather(hidden_block, "dp", axis=0, tiled=True)
    else:
        gathered = lax.all_gather(hidden_block, "tensor", axis=0, tiled=True)

    def model_term():
        return multiply_rows(matrix, transposed, gathered)

    if first:
        return lax.psum_scatter(model_term(), "tensor", scatter_dimension=0, tiled=True)
    return lax.psum_scatter(model_term(), "dp", scatter_dimension=0, tiled=True)


def normalize(activations, gain_row, shift_row, first):
    as_float = activations.astype(jnp.float32)
    summed = feature_total(jnp.sum(as_float, 1), first)
    average = summed / D
    centered = as_float - average[:, None]
    variance = feature_total(jnp.sum(centered * centered, 1), first) / D
    inverse_dev = lax.rsqrt(variance + epsilon)
    unit_rows = centered * inverse_dev[:, None]
    normalized = (unit_rows * gain_row + shift_row).astype(jnp.bfloat16)
    return (as_float, normalized, unit_rows, inverse_dev)


def forward(activations, params, first):
    gain_row, shift_row, up_matrix, up_row, down_matrix, down_row = params
    as_float, normalized, unit_rows, inverse_dev = normalize(
        activations, gain_row, shift_row, first
    )
    pre_act = to_hidden(normalized, up_matrix, False, first) + up_row
    hidden = gelu_value(pre_act).astype(jnp.bfloat16)
    mixed = to_model(hidden, down_matrix, False, first)
    output = (as_float + mixed + down_row).astype(jnp.bfloat16)
    return (output, (pre_act, unit_rows, inverse_dev))


def backward(incoming, saved, params, first):
    gain_row, shift_row, up_matrix, up_row, down_matrix, down_row = params
    pre_act, unit_rows, inverse_dev = saved
    hidden_grad = to_hidden(incoming, down_matrix, True, first)
    pre_grad = (hidden_grad * gelu_slope(pre_act)).astype(jnp.bfloat16)
    norm_grad = to_model(pre_grad, up_matrix, True, first)
    scaled = norm_grad * gain_row
    first_sum, second_sum = feature_total(
        (jnp.sum(scaled, 1), jnp.sum(scaled * unit_rows, 1)), first
    )
    first_mean = (first_sum / D)[:, None]
    second_mean = (second_sum / D)[:, None]
    result = incoming.astype(jnp.float32) + inverse_dev[:, None] * (
        scaled - first_mean - unit_rows * second_mean
    )
    return result.astype(jnp.bfloat16)


def section_params(first, norm_gain, norm_shift, up_weight, up_bias, down_weight, down_bias):
    features = up_weight.shape[1]
    units = up_weight.shape[2]
    if first:
        width_index = lax.axis_index("dp")
        unit_index = lax.axis_index("tensor")
    else:
        width_index = lax.axis_index("tensor")
        unit_index = lax.axis_index("dp")
    gain_row = lax.dynamic_slice_in_dim(norm_gain[0], width_index * features, features, 0)
    shift_row = lax.dynamic_slice_in_dim(norm_shift[0], width_index * features, features, 0)
    down_row = lax.dynamic_slice_in_dim(down_bias[0], width_index * features, features, 0)
    up_row = lax.dynamic_slice_in_dim(up_bias[0], unit_index * units, units, 0)
    return (gain_row, shift_row, up_weight[0], up_row, down_weight[0], down_row)


def to_second(block):
    return lax.all_to_all(
        lax.all_to_all(block, "dp", split_axis=0, concat_axis=1, tiled=True),
        "tensor",
        split_axis=1,
        concat_axis=0,
        tiled=True,
    )


def to_first(block):
    return lax.all_to_all(
        lax.all_to_all(block, "tensor", split_axis=0, concat_axis=1, tiled=True),
        "dp",
        split_axis=1,
        concat_axis=0,
        tiled=True,
    )


def send_forward(block):
    return passed_along(block, "section", 1)


def send_backward(block):
    return passed_along(block, "section", -1)


def shards(tokens, out_grad, norm_gain, norm_shift, up_weight, up_bias, down_weight, down_bias):
    section_index = lax.axis_index("section")
    first_params = section_params(
        True, norm_gain, norm_shift, up_weight, up_bias, down_weight, down_bias
    )
    second_params = section_params(
        False, norm_gain, norm_shift, up_weight, up_bias, down_weight, down_bias
    )
    first_out, first_saved = forward(tokens, first_params, True)
    second_in = to_second(send_forward(first_out))
    second_out, second_saved = forward(second_in, second_params, False)
    second_grad = backward(out_grad, second_saved, second_params, False)
    first_in = to_first(send_backward(second_grad))
    first_grad = backward(first_in, first_saved, first_params, True)
    first_section = section_index == 0
    outputs = jnp.where(first_section, first_out, second_out)[None]
    gradients = jnp.where(first_section, first_grad, second_grad)[None]
    return (outputs, gradients)


def solution(mesh):
    placed = (
        P("tensor", "dp"),
        P("tensor", "dp"),
        P("section", None),
        P("section", None),
        P("section", "dp", "tensor"),
        P("section", None),
        P("section", "tensor", "dp"),
        P("section", None),
    )
    return jax.shard_map(
        shards,
        mesh=mesh,
        in_specs=placed,
        out_specs=(P("section", "tensor", "dp"), P("section", "tensor", "dp")),
        check_vma=False,
    )
```

profile of v0, /device:TPU:1, one launch (start us, length us, event | category | flops | bytes accessed | tf_op | source)
XLA Modules:
  0.0 825.5 jit_solution(6940603904969036988)
XLA Ops:
  8.2 13.2 %psum.56 = f32[32]{0:T(128)S(1)} all-reduce(f32[32]{0:T(128)S(1)} %convert_reduce_fusion), channel_id=1, replica_groups=mesh['section'=2,'dp'=8,'tensor'=8] {'dp'}, use_global_device_ids=true, to_apply=%region_1.0 | all-reduce | flops 32 | bytes 256 | tf_op jit(solution)/shard_map/psum | solution.py:35
  22.5 14.7 %psum.57 = f32[32]{0:T(128)S(1)} all-reduce(f32[32]{0:T(128)S(1)} %fusion.42), channel_id=1, replica_groups=mesh['section'=2,'dp'=8,'tensor'=8] {'dp'}, use_global_device_ids=true, to_apply=%region_3.0 | all-reduce | flops 32 | bytes 256 | tf_op jit(solution)/shard_map/psum | solution.py:35
  39.0 31.1 %all_gather.24 = bf16[256,1536]{1,0:T(8,128)(2,1)S(1)} all-gather(bf16[32,1536]{1,0:T(8,128)(2,1)S(1)} %fusion.36), channel_id=1, replica_groups=mesh['section'=2,'dp'=8,'tensor'=8] {'tensor'}, dimensions={0}, use_global_device_ids=true | all-gather | bytes 884736 | tf_op jit(solution)/shard_map/all_gather | solution.py:49
  79.0 36.5 %reduce-scatter.9.cloned.1.call-done = f32[32,3072]{1,0:T(8,128)} async-done(((f32[256,3072]{1,0:T(8,128)}), f32[32,3072]{1,0:T(8,128)}) %reduce-scatter.9.cloned.1.call-update) | async-done | bytes 393232 | tf_op jit(solution)/shard_map/reduce_scatter | solution.py:57
  117.4 26.8 %all-gather.5.cloned.1.call-done = bf16[256,3072]{1,0:T(8,128)(2,1)} async-done(((bf16[32,3072]{1,0:T(8,128)(2,1)}), bf16[256,3072]{1,0:T(8,128)(2,1)}) %all-gather.5.cloned.1.call-update) | async-done | bytes 1572880 | tf_op jit(solution)/shard_map/all_gather | solution.py:63
  152.2 13.6 %all_gather.28 = bf16[256,1536]{1,0:T(8,128)(2,1)S(1)} all-gather(bf16[32,1536]{1,0:T(8,128)(2,1)S(1)} %copy-done.2), channel_id=1, replica_groups=mesh['section'=2,'dp'=8,'tensor'=8] {'dp'}, dimensions={0}, use_global_device_ids=true | all-gather | bytes 884736 | tf_op jit(solution)/shard_map/all_gather | solution.py:51
  174.6 50.7 %reduce-scatter.11.cloned.1.call-done = f32[32,1536]{1,0:T(8,128)} async-done(((f32[256,1536]{1,0:T(8,128)}), f32[32,1536]{1,0:T(8,128)}) %reduce-scatter.11.cloned.1.call-update) | async-done | bytes 196624 | tf_op jit(solution)/shard_map/reduce_scatter | solution.py:71
  230.2 11.6 %all_to_all.58 = bf16[8,4,1536]{2,1,0:T(4,128)(2,1)S(1)} all-to-all(bf16[8,4,1536]{2,1,0:T(4,128)(2,1)S(1)} %all_to_all.44), channel_id=1, replica_groups=mesh['section'=2,'dp'=8,'tensor'=8] {'dp'}, dimensions={0} | all-to-all | bytes 196608 | tf_op jit(solution)/shard_map/all_to_all | solution.py:135
  241.8 11.5 %all_to_all.59 = bf16[4,8,1536]{2,0,1:T(4,128)(2,1)S(1)} all-to-all(bf16[4,8,1536]{2,0,1:T(4,128)(2,1)S(1)} %bitcast.41), channel_id=1, replica_groups=mesh['section'=2,'dp'=8,'tensor'=8] {'tensor'}, dimensions={1} | all-to-all | bytes 196608 | tf_op jit(solution)/shard_map/all_to_all | solution.py:134
  253.5 17.6 %psum.58 = f32[32]{0:T(128)S(1)} all-reduce(f32[32]{0:T(128)S(1)} %reduce_sum.79), channel_id=1, replica_groups=mesh['section'=2,'dp'=8,'tensor'=8] {'tensor'}, use_global_device_ids=true, to_apply=%region_7.0 | all-reduce | flops 32 | bytes 256 | tf_op jit(solution)/shard_map/psum | solution.py:36
  271.6 16.9 %psum.59 = f32[32]{0:T(128)S(1)} all-reduce(f32[32]{0:T(128)S(1)} %reduce_sum.81), channel_id=1, replica_groups=mesh['section'=2,'dp'=8,'tensor'=8] {'tensor'}, use_global_device_ids=true, to_apply=%region_9.0 | all-reduce | flops 32 | bytes 256 | tf_op jit(solution)/shard_map/psum | solution.py:36
  288.6 22.5 %all_gather.26 = bf16[256,1536]{1,0:T(8,128)(2,1)S(1)} all-gather(bf16[32,1536]{1,0:T(8,128)(2,1)S(1)} %add_convert_fusion.2), channel_id=1, replica_groups=mesh['section'=2,'dp'=8,'tensor'=8] {'dp'}, dimensions={0}, use_global_device_ids=true | all-gather | bytes 884736 | tf_op jit(solution)/shard_map/all_gather | solution.py:51
  319.4 75.1 %reduce-scatter.13.cloned.1.call-done = f32[32,3072]{1,0:T(8,128)} async-done(((f32[256,3072]{1,0:T(8,128)}), f32[32,3072]{1,0:T(8,128)}) %reduce-scatter.13.cloned.1.call-update) | async-done | bytes 393232 | tf_op jit(solution)/shard_map/reduce_scatter | solution.py:58
  396.9 49.6 %all-gather.9.cloned.1.call-done = bf16[256,3072]{1,0:T(8,128)(2,1)} async-done(((bf16[32,3072]{1,0:T(8,128)(2,1)}), bf16[256,3072]{1,0:T(8,128)(2,1)}) %all-gather.9.cloned.1.call-update) | async-done | bytes 1572880 | tf_op jit(solution)/shard_map/all_gather | solution.py:65
  454.6 30.1 %reduce-scatter.19.cloned.1.call-done = f32[32,1536]{1,0:T(8,128)} async-done(((f32[256,1536]{1,0:T(8,128)}), f32[32,1536]{1,0:T(8,128)}) %reduce-scatter.19.cloned.1.call-update) | async-done | bytes 196624 | tf_op jit(solution)/shard_map/reduce_scatter | solution.py:72
  485.9 20.7 %all-reduce = (f32[32]{0:T(128)S(1)}, f32[32]{0:T(128)S(1)}) all-reduce(f32[32]{0:T(128)S(1)} %get-tuple-element.5, f32[32]{0:T(128)S(1)} %get-tuple-element.4), channel_id=1, replica_groups=mesh['section'=2,'dp'=8,'tensor'=8] {'tensor'}, use_global_device_ids=true, to_apply=%region_17.0 | all-reduce | flops 64 | bytes 512 | tf_op jit(solution)/shard_map/psum | solution.py:36
  522.2 16.5 %all_to_all.61 = bf16[4,8,1536]{2,0,1:T(4,128)(2,1)S(1)} all-to-all(bf16[4,8,1536]{2,0,1:T(4,128)(2,1)S(1)} %bitcast.42), channel_id=1, replica_groups=mesh['section'=2,'dp'=8,'tensor'=8] {'dp'}, dimensions={1} | all-to-all | bytes 196608 | tf_op jit(solution)/shard_map/all_to_all | solution.py:144
  538.8 30.2 %all_gather.30 = bf16[256,1536]{1,0:T(8,128)(2,1)S(1)} all-gather(bf16[32,1536]{1,0:T(8,128)(2,1)S(1)} %all_to_all.53), channel_id=1, replica_groups=mesh['section'=2,'dp'=8,'tensor'=8] {'tensor'}, dimensions={0}, use_global_device_ids=true | all-gather | bytes 884736 | tf_op jit(solution)/shard_map/all_gather | solution.py:49
  577.7 33.4 %reduce-scatter.21.cloned.1.call-done = f32[32,3072]{1,0:T(8,128)} async-done(((f32[256,3072]{1,0:T(8,128)}), f32[32,3072]{1,0:T(8,128)}) %reduce-scatter.21.cloned.1.call-update) | async-done | bytes 393232 | tf_op jit(solution)/shard_map/reduce_scatter | solution.py:57
  613.1 51.9 %all-gather.7.cloned.1.call-done = bf16[256,3072]{1,0:T(8,128)(2,1)} async-done(((bf16[32,3072]{1,0:T(8,128)(2,1)}), bf16[256,3072]{1,0:T(8,128)(2,1)}) %all-gather.7.cloned.1.call-update) | async-done | bytes 1572880 | tf_op jit(solution)/shard_map/all_gather | solution.py:65
  673.0 18.6 %all-gather.11.cloned.1.call-done = bf16[256,3072]{1,0:T(8,128)(2,1)} async-done(((bf16[32,3072]{1,0:T(8,128)(2,1)}), bf16[256,3072]{1,0:T(8,128)(2,1)}) %all-gather.11.cloned.1.call-update) | async-done | bytes 1572880 | tf_op jit(solution)/shard_map/all_gather | solution.py:63
  699.6 24.0 %reduce-scatter.15.cloned.1.call-done = f32[32,1536]{1,0:T(8,128)} async-done(((f32[256,1536]{1,0:T(8,128)}), f32[32,1536]{1,0:T(8,128)}) %reduce-scatter.15.cloned.1.call-update) | async-done | bytes 196624 | tf_op jit(solution)/shard_map/reduce_scatter | solution.py:72
  725.3 76.9 %reduce-scatter.23.cloned.1.call-done = f32[32,1536]{1,0:T(8,128)} async-done(((f32[256,1536]{1,0:T(8,128)}), f32[32,1536]{1,0:T(8,128)}) %reduce-scatter.23.cloned.1.call-update) | async-done | bytes 196624 | tf_op jit(solution)/shard_map/reduce_scatter | solution.py:71
  803.3 13.6 %all-reduce.1 = (f32[32]{0:T(128)S(1)}, f32[32]{0:T(128)S(1)}) all-reduce(f32[32]{0:T(128)S(1)} %get-tuple-element.3, f32[32]{0:T(128)S(1)} %get-tuple-element.2), channel_id=1, replica_groups=mesh['section'=2,'dp'=8,'tensor'=8] {'dp'}, use_global_device_ids=true, to_apply=%region_23.0 | all-reduce | flops 64 | bytes 512 | tf_op jit(solution)/shard_map/psum | solution.py:35
  (78 shorter events, 103.8 us)
Async XLA Ops:
  7.2 108.3 %reduce-scatter.9.cloned.1.call-start = ((), (), s32[]{:S(2)}) async-start(), calls=%async_computation.12 | async-start | bytes 3538944 | tf_op jit(solution)/shard_map/reduce_scatter | solution.py:57
  78.2 66.0 %all-gather.5.cloned.1.call-start = ((), (), s32[]{:S(2)}) async-start(), calls=%async_computation.13 | async-start | bytes 1769472 | tf_op jit(solution)/shard_map/all_gather | solution.py:63
  117.3 34.8 %copy-start.2 = (bf16[32,1536]{1,0:T(8,128)(2,1)S(1)}, bf16[32,1536]{1,0:T(8,128)(2,1)}, u32[]{:S(2)}) copy-start(bf16[32,1536]{1,0:T(8,128)(2,1)} %param.9) | copy-start | bytes 294916
  117.3 108.0 %reduce-scatter.11.cloned.1.call-start = ((), (), s32[]{:S(2)}) async-start(), calls=%async_computation.14 | async-start | bytes 1769472 | tf_op jit(solution)/shard_map/reduce_scatter | solution.py:71
  152.1 167.3 %reduce-scatter.17.cloned.1.call-start = ((), (), s32[]{:S(2)}) async-start(), calls=%async_computation.18 | async-start | bytes 3538944 | tf_op jit(solution)/shard_map/reduce_scatter | solution.py:58
  173.7 51.5 %copy-start = (bf16[32,1536]{1,0:T(8,128)(2,1)S(1)}, bf16[32,1536]{1,0:T(8,128)(2,1)}, u32[]{:S(2)}) copy-start(bf16[32,1536]{1,0:T(8,128)(2,1)} %param.8) | copy-start | bytes 294916
  173.8 220.7 %reduce-scatter.13.cloned.1.call-start = ((), (), s32[]{:S(2)}) async-start(), calls=%async_computation.15 | async-start | bytes 3538944 | tf_op jit(solution)/shard_map/reduce_scatter | solution.py:58
  226.3 3.9 collective-permute-start
  319.3 127.3 %all-gather.9.cloned.1.call-start = ((), (), s32[]{:S(2)}) async-start(), calls=%async_computation.19 | async-start | bytes 1769472 | tf_op jit(solution)/shard_map/all_gather | solution.py:65
  396.7 88.0 %reduce-scatter.19.cloned.1.call-start = ((), (), s32[]{:S(2)}) async-start(), calls=%async_computation.20 | async-start | bytes 1769472 | tf_op jit(solution)/shard_map/reduce_scatter | solution.py:72
  454.5 156.6 %reduce-scatter.21.cloned.1.call-start = ((), (), s32[]{:S(2)}) async-start(), calls=%async_computation.21 | async-start | bytes 3538944 | tf_op jit(solution)/shard_map/reduce_scatter | solution.py:57
  507.6 5.6 collective-permute-start.1
  576.9 34.2 %copy-start.1 = (f32[32,3072]{1,0:T(8,128)S(1)}, f32[32,3072]{1,0:T(8,128)}, u32[]{:S(2)}) copy-start(f32[32,3072]{1,0:T(8,128)} %reduce-scatter.9.cloned.1.call-done) | copy-start | bytes 1179652
  576.9 88.1 %all-gather.7.cloned.1.call-start = ((), (), s32[]{:S(2)}) async-start(), calls=%async_computation.16 | async-start | bytes 1769472 | tf_op jit(solution)/shard_map/all_gather | solution.py:65
  577.7 114.0 %all-gather.11.cloned.1.call-start = ((), (), s32[]{:S(2)}) async-start(), calls=%async_computation.22 | async-start | bytes 1769472 | tf_op jit(solution)/shard_map/all_gather | solution.py:63
  613.1 110.6 %reduce-scatter.15.cloned.1.call-start = ((), (), s32[]{:S(2)}) async-start(), calls=%async_computation.17 | async-start | bytes 1769472 | tf_op jit(solution)/shard_map/reduce_scatter | solution.py:72
  673.0 129.2 %reduce-scatter.23.cloned.1.call-start = ((), (), s32[]{:S(2)}) async-start(), calls=%async_computation.23 | async-start | bytes 1769472 | tf_op jit(solution)/shard_map/reduce_scatter | solution.py:71
Sparse Core Ops, SparseCore 0:
  78.3 37.1 reduce-scatter.8
  117.4 26.6 all-gather.4
  152.2 73.0 reduce-scatter.10
  229.1 79.1 reduce-scatter.16
  319.4 75.0 reduce-scatter.12
  396.8 49.7 all-gather.8
  454.7 30.0 reduce-scatter.18
  577.1 33.9 reduce-scatter.20
  613.4 51.5 all-gather.6
  666.6 25.0 all-gather.10
  694.1 29.5 reduce-scatter.14
  727.2 74.8 reduce-scatter.22
where the time goes:
time: 827 us; the launch traced here: 825 us
  waiting for transfers between devices  481 us (58%)
  blocking collectives  243 us (29%)
  matrix products  63.9 us (8%)
  other arithmetic  17.1 us (2%)
  between operations  14.3 us (2%)
    reduce_scatter x2, waiting for transfers between devices, to_model(): lax.psum_scatter(model_term(), 'tensor', scatter_dimension=0, tiled=True)  128 us
    all_gather x2, waiting for transfers between devices, to_model(): gathered = lax.all_gather(hidden_block, 'tensor', axis=0, tiled=True)  102 us
    reduce_scatter x2, waiting for transfers between devices, to_hidden(): lax.psum_scatter(hidden_term(), 'tensor', scatter_dimension=0, tiled=True)  75.1 us
    reduce_scatter x2, waiting for transfers between devices, to_hidden(): lax.psum_scatter(hidden_term(), 'dp', scatter_dimension=0, tiled=True)  69.9 us
    all_gather x2, blocking collectives, to_hidden(): gathered = lax.all_gather(row_block, 'tensor', axis=0, tiled=True)  61.2 us
    psum x3, blocking collectives, feature_total(): return lax.psum(values, 'tensor')  55.1 us
    reduce_scatter x2, waiting for transfers between devices, to_model(): return lax.psum_scatter(model_term(), 'dp', scatter_dimension=0, tiled=True)  54.2 us
    all_gather x2, waiting for transfers between devices, to_model(): gathered = lax.all_gather(hidden_block, 'dp', axis=0, tiled=True)  45.4 us
  transfers between devices with their start and end apart: 14, of which 13 were waited for; matrix products, arithmetic and copies ran while one was open for 5% of the time, Pallas kernels for 0%

commit v1 on v0

v1 whole, which is shorter than its diff:
```python
import functools

import jax
import jax.numpy as jnp
from jax import lax
from jax.experimental import pallas as pl
from jax.experimental.pallas import tpu as pltpu
from jax.sharding import PartitionSpec as P

D = 12288
ROWS = 32
MODEL = 1536
UNITS = 3072
N_CHUNKS, N_WIDTH = 3, 1024
M_CHUNKS, M_WIDTH = 3, 512
MESH = pl.DeviceIdType.MESH
F32, BF16 = jnp.float32, jnp.bfloat16

epsilon = 1e-05
root_scale = 0.7978845608028654
cubic_term = 0.044715


def gelu_value(pre_act):
    inner = root_scale * (pre_act + cubic_term * pre_act * pre_act * pre_act)
    return 0.5 * pre_act * (1.0 + jnp.tanh(inner))


def gelu_slope(pre_act):
    inner = root_scale * (pre_act + cubic_term * pre_act * pre_act * pre_act)
    tangent = jnp.tanh(inner)
    return 0.5 * (1.0 + tangent) + 0.5 * pre_act * (1.0 - tangent * tangent) * root_scale * (
        1.0 + 3.0 * cubic_term * pre_act * pre_act
    )


SEM_NAMES = {}


def sem_index(name, count=1):
    if name not in SEM_NAMES:
        SEM_NAMES[name] = sum(width for _, width in SEM_NAMES.values()), count
    return SEM_NAMES[name][0]


SEM_COUNT = 160


class Group:
    def __init__(self, section, axis, d, t):
        self.axis, self.section, self.d, self.t = axis, section, d, t
        self.index = d if axis == "dp" else t
        self.hi, self.lo = self.index // 2, self.index % 2

    def member(self, index):
        if self.axis == "dp":
            return (self.section, index, self.t)
        return (self.section, self.d, index)

    def at(self, hi, lo):
        return self.member(hi * 2 + lo)

    def pair(self):
        return self.at(self.hi, 1 - self.lo)


class Links:
    def __init__(self, sems):
        self.sems = sems
        self.sent = []

    def sem(self, name, offset=0, count=1):
        return self.sems.at[sem_index(name, count) + offset]

    def send(self, src, dst, to, send_sem, recv_sem):
        pltpu.make_async_remote_copy(
            src_ref=src, dst_ref=dst, send_sem=send_sem, recv_sem=recv_sem,
            device_id=to, device_id_type=MESH,
        ).start()

    def wait_recv(self, ref, sem, peer):
        pltpu.make_async_remote_copy(
            src_ref=ref, dst_ref=ref, send_sem=sem, recv_sem=sem,
            device_id=peer, device_id_type=MESH,
        ).wait_recv()

    def later(self, ref, sem, peer):
        self.sent.append((ref, sem, peer))

    def finish(self):
        for ref, sem, peer in self.sent:
            pltpu.make_async_remote_copy(
                src_ref=ref, dst_ref=ref, send_sem=sem, recv_sem=sem,
                device_id=peer, device_id_type=MESH,
            ).wait_send()
        self.sent = []


class Scatter:
    def __init__(self, links, group, name, part, from_pair, pair_sum, from_four):
        self.links, self.group, self.name = links, group, name
        self.part, self.from_pair, self.pair_sum, self.from_four = part, from_pair, pair_sum, from_four

    def send_pair(self, c):
        g, k = self.group, self.links
        src = self.part.at[c, :, 1 - g.lo]
        sem = k.sem(f"{self.name}/pair_send{c}")
        k.send(src, self.from_pair.at[c], g.pair(), sem, k.sem(f"{self.name}/pair_recv{c}"))
        k.later(src, sem, g.pair())

    def middle(self, c):
        g, k = self.group, self.links
        k.wait_recv(self.from_pair.at[c], k.sem(f"{self.name}/pair_recv{c}"), g.pair())
        total = self.part[c, :, g.lo].astype(F32) + self.from_pair[c].astype(F32)
        self.pair_sum[c] = total.astype(BF16)
        send_sem = k.sem(f"{self.name}/four_send{c}")
        for step in (2, 1, 3):
            to = (g.hi + step) % 4
            k.send(
                self.pair_sum.at[c, to], self.from_four.at[c, step - 1], g.at(to, g.lo),
                send_sem, k.sem(f"{self.name}/four_recv{c}"),
            )
        k.later(self.from_four.at[c], send_sem, g.pair())

    def finish(self, c):
        g, k = self.group, self.links
        k.wait_recv(self.from_four.at[c], k.sem(f"{self.name}/four_recv{c}"), g.pair())
        total = self.part[c, g.hi, g.lo].astype(F32) + self.from_pair[c, g.hi].astype(F32)
        for step in range(3):
            total = total + self.from_four[c, step].astype(F32)
        return total


class Gather:
    def __init__(self, links, group, name, whole):
        self.links, self.group, self.name, self.whole = links, group, name, whole

    def send(self, c):
        g, k = self.group, self.links
        own = self.whole.at[c, g.hi, g.lo]
        send_sem = k.sem(f"{self.name}/own_send{c}")
        for step in (2, 1, 3):
            k.send(own, own, g.at((g.hi + step) % 4, g.lo), send_sem,
                   k.sem(f"{self.name}/four_recv{c}", step - 1, 3))
        k.send(own, own, g.pair(), send_sem, k.sem(f"{self.name}/pair_recv{c}"))
        k.later(self.whole.at[c, :, g.lo], send_sem, g.pair())

    def forward(self, c):
        g, k = self.group, self.links
        send_sem = k.sem(f"{self.name}/on_send{c}")
        for step in (1, 3, 2):
            block = self.whole.at[c, (g.hi + 4 - step) % 4, g.lo]
            k.wait_recv(block, k.sem(f"{self.name}/four_recv{c}", step - 1, 3), g.pair())
            k.send(block, block, g.pair(), send_sem, k.sem(f"{self.name}/pair_recv{c}"))
        k.later(self.whole.at[c, pl.ds(0, 3), g.lo], send_sem, g.pair())

    def ready(self, c):
        g, k = self.group, self.links
        k.wait_recv(self.whole.at[c, :, 1 - g.lo], k.sem(f"{self.name}/pair_recv{c}"), g.pair())


class Cross:
    def __init__(self, links, group, name, whole, partners):
        self.links, self.group, self.name, self.whole, self.partners = links, group, name, whole, partners

    def send(self, source, four):
        g, k = self.group, self.links
        send_sem = k.sem(f"{self.name}/send")
        for to in self.partners:
            k.send(source, self.whole.at[g.hi, g.lo], to, send_sem, k.sem(f"{self.name}/recv", g.hi, 4))
        k.later(four, send_sem, g.pair())

    def receive(self):
        g, k = self.group, self.links
        send_sem = k.sem(f"{self.name}/on_send")
        for hi in range(4):
            block = self.whole.at[hi, g.lo]
            k.wait_recv(block, k.sem(f"{self.name}/recv", hi, 4), g.pair())
            k.send(block, block, g.pair(), send_sem, k.sem(f"{self.name}/pair_recv"))
        k.later(self.whole.at[:, g.lo], send_sem, g.pair())

    def ready(self):
        g, k = self.group, self.links
        k.wait_recv(self.whole.at[:, 1 - g.lo], k.sem(f"{self.name}/pair_recv"), g.pair())


def exchange(links, group, name, table):
    send_sem, recv_sem = links.sem(f"{name}/send"), links.sem(f"{name}/recv")
    for step in (4, 3, 5, 2, 6, 7, 1):
        links.send(table.at[0], table.at[step], group.member((group.index + step) % 8), send_sem, recv_sem)
    links.later(table.at[pl.ds(1, 7)], send_sem, group.pair())


def exchanged(links, group, name, table):
    links.wait_recv(table.at[pl.ds(1, 7)], links.sem(f"{name}/recv"), group.pair())


def two_lanes(first, second):
    lane = lax.broadcasted_iota(jnp.int32, (ROWS, 128), 1)
    return jnp.where(lane < 64, first, second)


def local_moments(values):
    average = jnp.sum(values, 1, keepdims=True) / MODEL
    centered = values - average
    return two_lanes(average, jnp.sum(centered * centered, 1, keepdims=True))


def combined_moments(table):
    average = table[0][:, 0:1]
    squares = table[0][:, 64:65]
    for k in range(1, 8):
        average = average + table[k][:, 0:1]
        squares = squares + table[k][:, 64:65]
    average = average / 8.0
    for k in range(8):
        offset = table[k][:, 0:1] - average
        squares = squares + MODEL * (offset * offset)
    return average, lax.rsqrt(squares / D + epsilon)


def added_lanes(table):
    total = table[0]
    for k in range(1, 8):
        total = total + table[k]
    return total[:, 0:1], total[:, 64:65]


def swap_matrix():
    row = lax.broadcasted_iota(jnp.int32, (256, 256), 0)
    column = lax.broadcasted_iota(jnp.int32, (256, 256), 1)
    source = ((row // 4) % 8) * 32 + (row // 32) * 4 + row % 4
    return jnp.where(column == source, 1.0, 0.0).astype(BF16)


def pick_matrix(q):
    row = lax.broadcasted_iota(jnp.int32, (ROWS, 256), 0)
    column = lax.broadcasted_iota(jnp.int32, (ROWS, 256), 1)
    return jnp.where(column == (row // 4) * 32 + q * 4 + row % 4, 1.0, 0.0)


def product(x, w_ref, transposed, k0, depth, n0, width):
    if transposed:
        return lax.dot_general(
            x, w_ref[pl.ds(n0, width), pl.ds(k0, depth)], (((1,), (1,)), ((), ())),
            preferred_element_type=F32,
        )
    return jnp.dot(x, w_ref[pl.ds(k0, depth), pl.ds(n0, width)], preferred_element_type=F32)


def kernel(
    tokens, out_grad, gain, shift, up, up_bias, down, down_bias, out_ref, grad_ref,
    U, V, gain_row, shift_row, up_row, down_row, xall, xn, xn2, part, from_pair, pair_sum, from_four,
    hall, acc, part_m, from_pair_m, pair_sum_m, from_four_m, pre, hidden_grad, moments, stats, sendbuf,
    own_stats, sems, local_sems,
):
    s, d, t = lax.axis_index("section"), lax.axis_index("dp"), lax.axis_index("tensor")

    barrier = pltpu.get_barrier_semaphore()
    cross_dp = jnp.where(s == 0, t % 2, t)
    cross_tensor = jnp.where(s == 0, d, d % 2)
    step_dp = jnp.where(s == 0, 2, 0)
    partners = [(1 - s, cross_dp + step_dp * k, cross_tensor + (2 - step_dp) * k) for k in range(4)]
    for k in range(1, 8):
        pl.semaphore_signal(barrier, inc=1, device_id=(s, (d + k) % 8, t), device_id_type=MESH)
        pl.semaphore_signal(barrier, inc=1, device_id=(s, d, (t + k) % 8), device_id_type=MESH)
    for to in partners:
        pl.semaphore_signal(barrier, inc=1, device_id=to, device_id_type=MESH)

    def fetch(src, dst, index):
        copy = pltpu.make_async_copy(src, dst, local_sems.at[index])
        copy.start()
        return copy

    def branch(section):
        first = section == 0
        links = Links(sems)
        hidden_group = Group(section, "dp" if first else "tensor", d, t)
        model_group = Group(section, "tensor" if first else "dp", d, t)
        width_index, unit_index = (d, t) if first else (t, d)
        features = pl.ds(pl.multiple_of(width_index * MODEL, MODEL), MODEL)
        units = pl.ds(pl.multiple_of(unit_index * UNITS, UNITS), UNITS)
        g = model_group
        own_x = xall.at[0, 0, g.hi, g.lo]
        get_own = fetch(tokens if first else out_grad, own_x, 0)
        weights = [(up.at[0], U, 1), (down.at[0], V, 2)]
        gets = {}
        for src, dst, index in weights if first else weights[::-1]:
            gets[index] = fetch(src, dst, index)
        small = [
            fetch(gain.at[:, features], gain_row, 3), fetch(shift.at[:, features], shift_row, 4),
            fetch(up_bias.at[:, units], up_row, 5), fetch(down_bias.at[:, features], down_row, 6),
        ]
        get_own.wait()
        pl.semaphore_wait(barrier, 18)

        def scatter_hidden(slot):
            return Scatter(links, hidden_group, f"h{slot}", part.at[slot], from_pair.at[slot],
                           pair_sum.at[slot], from_four.at[slot])

        def scatter_model(slot):
            return Scatter(links, model_group, f"m{slot}", part_m.at[slot], from_pair_m.at[slot],
                           pair_sum_m.at[slot], from_four_m.at[slot])

        def gather_hidden(slot):
            return Gather(links, hidden_group, f"g{slot}", hall.at[slot])

        def start_hidden(x_ref, w_ref, transposed, scatter):
            for c in range(N_CHUNKS):
                @pl.loop(0, N_WIDTH // 512)
                def _(n):
                    at = pl.multiple_of(n * 512, 512)
                    x = x_ref[...].reshape(256, MODEL)
                    value = product(x, w_ref, transposed, 0, MODEL, pl.multiple_of(c * N_WIDTH + n * 512, 512), 512)
                    scatter.part[c, :, :, :, pl.ds(at, 512)] = value.astype(BF16).reshape(4, 2, ROWS, 512)

                scatter.send_pair(c)
                if c >= 1:
                    scatter.middle(c - 1)
            scatter.middle(N_CHUNKS - 1)

        def to_model(gather, c, w_ref, transposed, scatter):
            gather.ready(c)
            if c < N_CHUNKS - 1:
                @pl.loop(0, MODEL // 512)
                def _(n):
                    at = pl.multiple_of(n * 512, 512)
                    x = gather.whole[c].reshape(256, N_WIDTH)
                    value = product(x, w_ref, transposed, c * N_WIDTH, N_WIDTH, at, 512)
                    if c == 0:
                        acc[:, pl.ds(at, 512)] = value
                    else:
                        acc[:, pl.ds(at, 512)] += value
                return
            for m in range(M_CHUNKS):
                at = m * M_WIDTH
                x = gather.whole[c].reshape(256, N_WIDTH)
                value = product(x, w_ref, transposed, c * N_WIDTH, N_WIDTH, at, M_WIDTH)
                value = value + acc[:, pl.ds(at, M_WIDTH)]
                scatter.part[m] = value.astype(BF16).reshape(4, 2, ROWS, M_WIDTH)
                scatter.send_pair(m)
                if m >= 1:
                    scatter.middle(m - 1)
            scatter.middle(M_CHUNKS - 1)

        def through(scatter, gather, epilogue, w_ref, transposed, scatter_out):
            for c in range(N_CHUNKS):
                if scatter is None:
                    value = epilogue(c, None)
                else:
                    value = epilogue(c, scatter.finish(c))
                gather.whole[c, hidden_group.hi, hidden_group.lo] = value.astype(BF16)
                gather.send(c)
                if c >= 1:
                    gather.forward(c - 1)
                if c >= 2:
                    to_model(gather, c - 2, w_ref, transposed, scatter_out)
            gather.forward(N_CHUNKS - 1)
            to_model(gather, N_CHUNKS - 2, w_ref, transposed, scatter_out)
            to_model(gather, N_CHUNKS - 1, w_ref, transposed, scatter_out)

        def finish_model(scatter):
            return jnp.concatenate([scatter.finish(m) for m in range(M_CHUNKS)], axis=1)

        def normalize_all(source):
            for hi in range(4):
                for lo in range(2):
                    average = stats[hi, lo][:, 0:1]
                    inverse_dev = stats[hi, lo][:, 64:65]
                    unit = (source[hi, lo].astype(F32) - average) * inverse_dev
                    xn[hi, lo] = (unit * gain_row[...] + shift_row[...]).astype(BF16)

        def unit_slice(c):
            return pl.ds(c * N_WIDTH, N_WIDTH)

        def input_gradient(incoming, norm_grad, unit, inverse_dev, slot):
            scaled = norm_grad * gain_row[...]
            group = hidden_group
            moments[slot, 0] = two_lanes(
                jnp.sum(scaled, 1, keepdims=True), jnp.sum(scaled * unit, 1, keepdims=True)
            )
            exchange(links, group, "sums", moments.at[slot])
            exchanged(links, group, "sums", moments.at[slot])
            first_sum, second_sum = added_lanes(moments.at[slot])
            return (incoming + inverse_dev * (scaled - first_sum / D - unit * (second_sum / D))).astype(BF16)

        tokens_gather = Gather(links, model_group, "x", xall.at[0])
        rows_across = Cross(links, model_group, "y0" if first else "g1", xall.at[1, 0], partners)
        rows_back = Cross(links, model_group, "g1" if first else "y0", xall.at[1, 0], partners)
        stats_cross = Cross(links, model_group, "y0stats", stats, partners)

        tokens_gather.send(0)
        if first:
            own = own_x[...].astype(F32)
            moments[0, 0] = local_moments(own)
            exchange(links, hidden_group, "0first", moments.at[0])
            exchanged(links, hidden_group, "0first", moments.at[0])
            average, inverse_dev = combined_moments(moments.at[0])
            own_stats[...] = two_lanes(average, inverse_dev)
            stats[g.hi, g.lo] = own_stats[...]
            for k in range(1, 8):
                place = stats.at[g.hi, g.lo]
                links.send(place, place, g.member((g.index + k) % 8), links.sem("0st/send"), links.sem("0st/recv"))
            links.later(moments.at[0, pl.ds(0, 7)], links.sem("0st/send"), g.pair())
            tokens_gather.forward(0)
            tokens_gather.ready(0)
            links.wait_recv(moments.at[0, pl.ds(0, 7)], links.sem("0st/recv"), g.pair())
            for copy in small:
                copy.wait()
            normalize_all(xall.at[0, 0])
            gets[1].wait()
            scatter = scatter_hidden(0)
            start_hidden(xn, U, False, scatter)
            gets[2].wait()

            def forward_hidden(c, value):
                value = value + up_row[:, unit_slice(c)]
                pre[:, unit_slice(c)] = value
                return gelu_value(value)

            scatter_out = scatter_model(0)
            through(scatter, gather_hidden(0), forward_hidden, V, False, scatter_out)
            mixed = finish_model(scatter_out)
            y0 = (own_x[...].astype(F32) + mixed + down_row[...]).astype(BF16)
            sendbuf[0] = y0
            rows_across.send(sendbuf.at[0], sendbuf)
            moments[1, 0] = local_moments(y0.astype(F32))
            exchange(links, hidden_group, "0second", moments.at[1])
            out_ref[0] = y0
            exchanged(links, hidden_group, "0second", moments.at[1])
            average, inverse_dev = combined_moments(moments.at[1])
            moments[3, 0] = two_lanes(average, inverse_dev)
            stats_cross.send(moments.at[3, 0], moments.at[3, pl.ds(0, 4)])

            rows_back.receive()
            rows_back.ready()
            xn2[...] = jnp.dot(
                swap_matrix(), xall[1, 0].reshape(256, MODEL), preferred_element_type=F32
            ).astype(BF16).reshape(4, 2, ROWS, MODEL)
            scatter = scatter_hidden(1)
            start_hidden(xn2, V, True, scatter)

            def backward_hidden(c, value):
                return value * gelu_slope(pre[:, unit_slice(c)])

            scatter_out = scatter_model(1)
            through(scatter, gather_hidden(1), backward_hidden, U, True, scatter_out)
            norm_grad = finish_model(scatter_out)
            average, inverse_dev = own_stats[:, 0:1], own_stats[:, 64:65]
            unit = (own_x[...].astype(F32) - average) * inverse_dev
            incoming = xn2[g.hi, g.lo].astype(F32)
            grad_ref[0] = input_gradient(incoming, norm_grad, unit, inverse_dev, 2)
        else:
            tokens_gather.forward(0)
            tokens_gather.ready(0)
            gets[2].wait()
            scatter = scatter_hidden(0)
            start_hidden(xall.at[0, 0], V, True, scatter)
            for c in range(N_CHUNKS):
                hidden_grad[:, unit_slice(c)] = scatter.finish(c)
            for copy in small:
                copy.wait()
            gets[1].wait()

            rows_back.receive()
            stats_cross.receive()
            rows_back.ready()
            stats_cross.ready()
            normalize_all(xall.at[1, 0])
            xn2[...] = jnp.dot(
                swap_matrix(), xn[...].reshape(256, MODEL), preferred_element_type=F32
            ).astype(BF16).reshape(4, 2, ROWS, MODEL)
            scatter = scatter_hidden(1)
            start_hidden(xn2, U, False, scatter)
            pick = pick_matrix(d)
            y0_own = jnp.dot(
                pick.astype(BF16), xall[1, 0].reshape(256, MODEL), preferred_element_type=F32
            )
            own_stats[...] = jnp.dot(
                pick, stats[...].reshape(256, 128), preferred_element_type=F32,
                precision=lax.Precision.HIGHEST,
            )

            def backward_hidden(c, value):
                value = value + up_row[:, unit_slice(c)]
                pre[:, unit_slice(c)] = value
                return hidden_grad[:, unit_slice(c)] * gelu_slope(value)

            scatter_out = scatter_model(0)
            through(scatter, gather_hidden(0), backward_hidden, U, True, scatter_out)
            norm_grad = finish_model(scatter_out)
            average, inverse_dev = own_stats[:, 0:1], own_stats[:, 64:65]
            unit = (y0_own - average) * inverse_dev
            g1 = input_gradient(own_x[...].astype(F32), norm_grad, unit, inverse_dev, 2)
            sendbuf[0] = g1
            rows_across.send(sendbuf.at[0], sendbuf)
            grad_ref[0] = g1

            def forward_hidden(c, value):
                return gelu_value(pre[:, unit_slice(c)])

            scatter_out = scatter_model(1)
            through(None, gather_hidden(1), forward_hidden, V, False, scatter_out)
            mixed = finish_model(scatter_out)
            out_ref[0] = (y0_own + mixed + down_row[...]).astype(BF16)
        links.finish()

    for section in range(2):
        pl.when(s == section)(functools.partial(branch, section))
    assert sum(width for _, width in SEM_NAMES.values()) <= SEM_COUNT


def shards(tokens, out_grad, norm_gain, norm_shift, up_weight, up_bias, down_weight, down_bias):
    vmem = pltpu.VMEM
    return pl.pallas_call(
        kernel,
        out_shape=[jax.ShapeDtypeStruct((1, ROWS, MODEL), BF16)] * 2,
        in_specs=[pl.BlockSpec(memory_space=pl.ANY)] * 8,
        out_specs=[pl.BlockSpec(memory_space=vmem)] * 2,
        scratch_shapes=[
            vmem((MODEL, UNITS), BF16),
            vmem((UNITS, MODEL), BF16),
            vmem((1, MODEL), F32),
            vmem((1, MODEL), F32),
            vmem((1, UNITS), F32),
            vmem((1, MODEL), F32),
            vmem((2, 1, 4, 2, ROWS, MODEL), BF16),
            vmem((4, 2, ROWS, MODEL), BF16),
            vmem((4, 2, ROWS, MODEL), BF16),
            vmem((2, N_CHUNKS, 4, 2, ROWS, N_WIDTH), BF16),
            vmem((2, N_CHUNKS, 4, ROWS, N_WIDTH), BF16),
            vmem((2, N_CHUNKS, 4, ROWS, N_WIDTH), BF16),
            vmem((2, N_CHUNKS, 3, ROWS, N_WIDTH), BF16),
            vmem((2, N_CHUNKS, 4, 2, ROWS, N_WIDTH), BF16),
            vmem((256, MODEL), F32),
            vmem((2, M_CHUNKS, 4, 2, ROWS, M_WIDTH), BF16),
            vmem((2, M_CHUNKS, 4, ROWS, M_WIDTH), BF16),
            vmem((2, M_CHUNKS, 4, ROWS, M_WIDTH), BF16),
            vmem((2, M_CHUNKS, 3, ROWS, M_WIDTH), BF16),
            vmem((ROWS, UNITS), F32),
            vmem((ROWS, UNITS), F32),
            vmem((4, 8, ROWS, 128), F32),
            vmem((4, 2, ROWS, 128), F32),
            vmem((4, ROWS, MODEL), BF16),
            vmem((ROWS, 128), F32),
            pltpu.SemaphoreType.DMA((SEM_COUNT,)),
            pltpu.SemaphoreType.DMA((8,)),
        ],
        compiler_params=pltpu.CompilerParams(
            collective_id=0, has_side_effects=True, vmem_limit_bytes=58 * 2**20
        ),
        cost_estimate=pl.CostEstimate(flops=10**10, bytes_accessed=2 * 10**7, transcendentals=10**5),
        name="relay",
    )(tokens, out_grad, norm_gain, norm_shift, up_weight, up_bias, down_weight, down_bias)


def solution(mesh):
    placed = (
        P("tensor", "dp"),
        P("tensor", "dp"),
        P("section", None),
        P("section", None),
        P("section", "dp", "tensor"),
        P("section", None),
        P("section", "tensor", "dp"),
        P("section", None),
    )
    return jax.shard_map(
        shards,
        mesh=mesh,
        in_specs=placed,
        out_specs=(P("section", "tensor", "dp"), P("section", "tensor", "dp")),
        check_vma=False,
    )
```

time: 827 us -> 216 us (0.26)
  waiting for transfers between devices: 481 us -> 0 us
  blocking collectives: 243 us -> 0 us
  Pallas kernels: 0 us -> 212 us
  matrix products: 63.9 us -> 0 us
  other arithmetic: 17.1 us -> 0 us
  between operations: 14.3 us -> 0.64 us
    reduce_scatter x8 -> x0, waiting for transfers between devices: 327 us -> none  [the longest x2 128 us: to_model(): lax.psum_scatter(model_term(), 'tensor', scatter_dimension=0, tiled=True)]
    pallas_call x0 -> x1, Pallas kernels: none -> 212 us  [shards(): pl.pallas_call(kernel, out_shape=[jax.ShapeDtypeStruct((1, ROWS, MODEL),...]
    all_gather x4 -> x0, waiting for transfers between devices: 147 us -> none  [the longest x2 102 us: to_model(): gathered = lax.all_gather(hidden_block, 'tensor', axis=0, tiled=True)]
    all_gather x4 -> x0, blocking collectives: 97.3 us -> none  [the longest x2 61.2 us: to_hidden(): gathered = lax.all_gather(row_block, 'tensor', axis=0, tiled=True)]
    psum x6 -> x0, blocking collectives: 96.6 us -> none  [the longest x3 55.1 us: feature_total(): return lax.psum(values, 'tensor')]
    dot_general x8 -> x0, matrix products: 63.9 us -> none  [the longest x4 32.1 us: multiply_rows(): return jnp.dot(row_block, matrix, preferred_element_type=jnp.float32)]
    all_to_all x4 -> x0, blocking collectives: 48.7 us -> none  [the longest x1 16.5 us: to_first(): lax.all_to_all(lax.all_to_all(block, 'tensor', split_axis=0, concat_axis=...]
    convert_element_type x8 -> x0, other arithmetic: 9.02 us -> none  [the longest x2 4.09 us: backward(): pre_grad = (hidden_grad * gelu_slope(pre_act)).astype(jnp.bfloat16)]
  transfers between devices with their start and end apart: 14 -> 0, of which waited for: 13 -> 0; matrix products, arithmetic and copies ran while one was open for 5% -> 0% of each run, Pallas kernels for 0% -> 0%
where the time goes in v1:
time: 216 us; the launch traced here: 215 us
  Pallas kernels  212 us (98%)
  local copies, waits for them, and re-layouts  3.08 us (1%)
    pallas_call x1, Pallas kernels, shards(): pl.pallas_call(kernel, out_shape=[jax.ShapeDtypeStruct((1, ROWS, MODEL),...  212 us

profile of v1, /device:TPU:1, one launch (start us, length us, event | category | flops | bytes accessed | tf_op | source)
XLA Modules:
  0.0 215.4 jit_solution(9321941382496884413)
XLA Ops:
  0.6 211.7 %relay.1 = (bf16[1,32,1536]{2,1,0:T(8,128)(2,1)}, bf16[1,32,1536]{2,1,0:T(8,128)(2,1)}) custom-call(bf16[32,1536]{1,0:T(8,128)(2,1)} %tokens.1, bf16[32,1536]{1,0:T(8,128)(2,1)} %out_grad.1, f32[1,12288]{1,0:T(1,128)} %gain.1, f32[1,12288]{1,0:T(1,128)} %shift.1, bf16[1,1536,3072]{2,1,0:T(8,128)(2,1)} %up.1, f32[1,24576]{1,0:T(1,128)} %up_bias.1, ...), custom_call_target="tpu_custom_call" | custom-call | flops 10000000000 | bytes 20000000 | tf_op jit(solution)/shard_map/relay/pallas_call | solution.py:515
  212.3 1.5 copy.12
  213.8 1.5 copy.13

commit v2 on v1

v2 whole, which is shorter than its diff:
```python
import functools

import jax
import jax.numpy as jnp
from jax import lax
from jax.experimental import pallas as pl
from jax.experimental.pallas import tpu as pltpu
from jax.sharding import PartitionSpec as P

D = 12288
ROWS = 32
MODEL = 1536
UNITS = 3072
HALVES = 2
BLOCK = ROWS // HALVES
HALF = 8 * BLOCK
N_CHUNKS, N_WIDTH = 2, 1536
M_CHUNKS, M_WIDTH = 1, 1536
FAR_FIRST = (4, 3, 5, 2, 6, 7, 1)
MESH = pl.DeviceIdType.MESH
F32, BF16 = jnp.float32, jnp.bfloat16

epsilon = 1e-05
root_scale = 0.7978845608028654
cubic_term = 0.044715


def gelu_value(pre_act):
    inner = root_scale * (pre_act + cubic_term * pre_act * pre_act * pre_act)
    return 0.5 * pre_act * (1.0 + jnp.tanh(inner))


def gelu_slope(pre_act):
    inner = root_scale * (pre_act + cubic_term * pre_act * pre_act * pre_act)
    tangent = jnp.tanh(inner)
    return 0.5 * (1.0 + tangent) + 0.5 * pre_act * (1.0 - tangent * tangent) * root_scale * (
        1.0 + 3.0 * cubic_term * pre_act * pre_act
    )


SEM_NAMES = {}


def sem_index(name, count=1):
    if name not in SEM_NAMES:
        SEM_NAMES[name] = sum(width for _, width in SEM_NAMES.values()), count
    return SEM_NAMES[name][0]


SEM_COUNT = 220


class Group:
    def __init__(self, section, axis, d, t):
        self.axis, self.section, self.d, self.t = axis, section, d, t
        self.index = d if axis == "dp" else t
        self.hi, self.lo = self.index // 2, self.index % 2

    def member(self, index):
        if self.axis == "dp":
            return (self.section, index, self.t)
        return (self.section, self.d, index)

    def at(self, hi, lo):
        return self.member(hi * 2 + lo)

    def pair(self):
        return self.at(self.hi, 1 - self.lo)


class Links:
    def __init__(self, sems):
        self.sems = sems
        self.sent = []

    def sem(self, name, offset=0, count=1):
        return self.sems.at[sem_index(name, count) + offset]

    def send(self, src, dst, to, send_sem, recv_sem):
        pltpu.make_async_remote_copy(
            src_ref=src, dst_ref=dst, send_sem=send_sem, recv_sem=recv_sem,
            device_id=to, device_id_type=MESH,
        ).start()

    def wait_recv(self, ref, sem, peer):
        pltpu.make_async_remote_copy(
            src_ref=ref, dst_ref=ref, send_sem=sem, recv_sem=sem,
            device_id=peer, device_id_type=MESH,
        ).wait_recv()

    def later(self, ref, sem, peer):
        self.sent.append((ref, sem, peer))

    def finish(self):
        for ref, sem, peer in self.sent:
            pltpu.make_async_remote_copy(
                src_ref=ref, dst_ref=ref, send_sem=sem, recv_sem=sem,
                device_id=peer, device_id_type=MESH,
            ).wait_send()
        self.sent = []


class PairScatter:
    def __init__(self, links, group, name, part, from_pair, pair_sum, received):
        self.links, self.group, self.name = links, group, name
        self.part, self.from_pair, self.pair_sum = part, from_pair, pair_sum
        self.received = received.at[pl.ds(0, 3)]

    def send(self):
        g, k = self.group, self.links
        src = self.part.at[:, 1 - g.lo]
        sem = k.sem(f"{self.name}/pair_send")
        k.send(src, self.from_pair, g.pair(), sem, k.sem(f"{self.name}/pair_recv"))
        k.later(src, sem, g.pair())

    def middle(self):
        g, k = self.group, self.links
        yield
        k.wait_recv(self.from_pair, k.sem(f"{self.name}/pair_recv"), g.pair())
        total = self.part[:, g.lo].astype(F32) + self.from_pair[...].astype(F32)
        self.pair_sum[...] = total.astype(BF16)
        send_sem = k.sem(f"{self.name}/send")
        for step in (2, 1, 3):
            to = (g.hi + step) % 4
            k.send(self.pair_sum.at[to], self.received.at[step - 1], g.at(to, g.lo), send_sem,
                   k.sem(f"{self.name}/recv"))
        k.later(self.received, send_sem, g.pair())

    def finish(self):
        g, k = self.group, self.links
        k.wait_recv(self.received, k.sem(f"{self.name}/recv"), g.pair())
        total = self.part[g.hi, g.lo].astype(F32) + self.from_pair[g.hi].astype(F32)
        for step in range(3):
            total = total + self.received[step].astype(F32)
        return total


class DirectScatter:
    def __init__(self, links, group, name, part, from_pair, pair_sum, received):
        self.links, self.group, self.name, self.part, self.received = links, group, name, part, received

    def send(self):
        g, k = self.group, self.links
        send_sem = k.sem(f"{self.name}/send")
        for step in FAR_FIRST:
            to = (g.index + step) % 8
            k.send(self.part.at[to // 2, to % 2], self.received.at[step - 1], g.member(to), send_sem,
                   k.sem(f"{self.name}/recv"))
        k.later(self.received, send_sem, g.pair())

    def middle(self):
        return
        yield

    def finish(self):
        g, k = self.group, self.links
        k.wait_recv(self.received, k.sem(f"{self.name}/recv"), g.pair())
        total = self.part[g.hi, g.lo].astype(F32)
        for step in range(7):
            total = total + self.received[step].astype(F32)
        return total


class PairGather:
    def __init__(self, links, group, name, whole, seven):
        self.links, self.group, self.name, self.whole = links, group, name, whole

    def send(self):
        g, k = self.group, self.links
        own = self.whole.at[g.hi, g.lo]
        send_sem = k.sem(f"{self.name}/send")
        for step in (2, 1, 3):
            k.send(own, own, g.at((g.hi + step) % 4, g.lo), send_sem, k.sem(f"{self.name}/recv", step - 1, 3))
        k.send(own, own, g.pair(), send_sem, k.sem(f"{self.name}/pair_recv"))
        k.later(self.whole.at[:, g.lo], send_sem, g.pair())

    def forward(self):
        g, k = self.group, self.links
        send_sem = k.sem(f"{self.name}/on_send")
        yield
        for step in (1, 3, 2):
            block = self.whole.at[(g.hi + 4 - step) % 4, g.lo]
            k.wait_recv(block, k.sem(f"{self.name}/recv", step - 1, 3), g.pair())
            k.send(block, block, g.pair(), send_sem, k.sem(f"{self.name}/pair_recv"))
        k.later(self.whole.at[pl.ds(0, 3), g.lo], send_sem, g.pair())

    def ready(self):
        g, k = self.group, self.links
        k.wait_recv(self.whole.at[:, 1 - g.lo], k.sem(f"{self.name}/pair_recv"), g.pair())


class DirectGather:
    def __init__(self, links, group, name, whole, seven):
        self.links, self.group, self.name, self.whole, self.seven = links, group, name, whole, seven

    def send(self):
        g, k = self.group, self.links
        own = self.whole.at[g.hi, g.lo]
        send_sem = k.sem(f"{self.name}/send")
        for step in FAR_FIRST:
            k.send(own, own, g.member((g.index + step) % 8), send_sem, k.sem(f"{self.name}/recv"))
        k.later(self.seven, send_sem, g.pair())

    def forward(self):
        return
        yield

    def ready(self):
        self.links.wait_recv(self.seven, self.links.sem(f"{self.name}/recv"), self.group.pair())


class Cross:
    def __init__(self, links, group, name, whole, partners):
        self.links, self.group, self.name, self.whole, self.partners = links, group, name, whole, partners

    def send(self, source, four):
        g, k = self.group, self.links
        send_sem = k.sem(f"{self.name}/send")
        for to in self.partners:
            k.send(source, self.whole.at[g.hi, g.lo], to, send_sem, k.sem(f"{self.name}/recv", g.hi, 4))
        k.later(four, send_sem, g.pair())

    def receive(self):
        g, k = self.group, self.links
        send_sem = k.sem(f"{self.name}/on_send")
        yield
        for hi in range(4):
            block = self.whole.at[hi, g.lo]
            k.wait_recv(block, k.sem(f"{self.name}/recv", hi, 4), g.pair())
            k.send(block, block, g.pair(), send_sem, k.sem(f"{self.name}/pair_recv"))
        k.later(self.whole.at[:, g.lo], send_sem, g.pair())

    def ready(self):
        g, k = self.group, self.links
        k.wait_recv(self.whole.at[:, 1 - g.lo], k.sem(f"{self.name}/pair_recv"), g.pair())


def exchange(links, group, name, table, combine):
    send_sem, recv_sem = links.sem(f"{name}/send"), links.sem(f"{name}/recv")
    for step in FAR_FIRST:
        links.send(table.at[0], table.at[step], group.member((group.index + step) % 8), send_sem, recv_sem)
    links.later(table.at[pl.ds(1, 7)], send_sem, group.pair())
    yield
    links.wait_recv(table.at[pl.ds(1, 7)], recv_sem, group.pair())
    return combine([table[k] for k in range(8)])


def pairwise(links, group, name, table, combine):
    pair_send, pair_recv = links.sem(f"{name}/pair_send"), links.sem(f"{name}/pair_recv")
    links.send(table.at[0], table.at[1], group.pair(), pair_send, pair_recv)
    links.later(table.at[0], pair_send, group.pair())
    yield
    links.wait_recv(table.at[1], pair_recv, group.pair())
    table[2] = combine([table[0], table[1]])
    send_sem, recv_sem = links.sem(f"{name}/send"), links.sem(f"{name}/recv")
    for step in (2, 1, 3):
        links.send(table.at[2], table.at[2 + step], group.at((group.hi + step) % 4, group.lo), send_sem, recv_sem)
    links.later(table.at[pl.ds(3, 3)], send_sem, group.pair())
    yield
    links.wait_recv(table.at[pl.ds(3, 3)], recv_sem, group.pair())
    return combine([table[k] for k in range(2, 6)])


def drive(chains):
    alive = list(chains)
    while alive:
        for chain in list(alive):
            try:
                next(chain)
            except StopIteration:
                alive.remove(chain)


def add_all(parts):
    return functools.reduce(lambda left, right: left + right, parts)


def join_moments(parts):
    averages = [part[:, 0:1] for part in parts]
    average = add_all(averages) / len(parts)
    squares = add_all([part[:, 64:65] for part in parts])
    spread = add_all([(one - average) * (one - average) for one in averages])
    return two_lanes(average, squares + (MODEL if len(parts) == 2 else 2 * MODEL) * spread)


def two_lanes(first, second):
    lane = lax.broadcasted_iota(jnp.int32, (BLOCK, 128), 1)
    return jnp.where(lane < 64, first, second)


def local_moments(values):
    average = jnp.sum(values, 1, keepdims=True) / MODEL
    centered = values - average
    return two_lanes(average, jnp.sum(centered * centered, 1, keepdims=True))


def row_stats(joined):
    return two_lanes(joined[:, 0:1], lax.rsqrt(joined[:, 64:65] / D + epsilon))


def selection(rows, columns, source):
    row = lax.broadcasted_iota(jnp.int32, (rows, columns), 0)
    column = lax.broadcasted_iota(jnp.int32, (rows, columns), 1)
    return jnp.where(column == source(row), 1.0, 0.0)


WITHIN = BLOCK // 8


def swap_matrix():
    return selection(HALF, HALF, lambda i: ((i // WITHIN) % 8) * BLOCK + (i // BLOCK) * WITHIN + i % WITHIN).astype(BF16)


def pick_matrix(q):
    return selection(BLOCK, HALF, lambda i: (i // WITHIN) * BLOCK + q * WITHIN + i % WITHIN)


def halves_matrix():
    return selection(ROWS, ROWS, lambda i: ((i % BLOCK) // WITHIN) * 4 + (i // BLOCK) * WITHIN + i % WITHIN).astype(BF16)


def whole_matrix():
    return selection(ROWS, ROWS, lambda i: ((i % 4) // WITHIN) * BLOCK + (i // 4) * WITHIN + i % WITHIN).astype(BF16)


def moved(matrix, rows):
    return jnp.dot(matrix, rows, preferred_element_type=F32).astype(BF16)


def product(x, w_ref, transposed, k0, depth, n0, width):
    if transposed:
        return lax.dot_general(
            x, w_ref[pl.ds(n0, width), pl.ds(k0, depth)], (((1,), (1,)), ((), ())),
            preferred_element_type=F32,
        )
    return jnp.dot(x, w_ref[pl.ds(k0, depth), pl.ds(n0, width)], preferred_element_type=F32)


def kernel(
    tokens, out_grad, gain, shift, up, up_bias, down, down_bias, out_ref, grad_ref,
    U, V, gain_row, shift_row, up_row, down_row, raw, xall, xn, xn2, part, from_pair, pair_sum, received,
    hall, acc, part_m, from_pair_m, pair_sum_m, received_m, pre, hidden_grad, moments, stats, cross_stats,
    sendbuf, gradbuf, y0_own, own_stats, sems, local_sems,
):
    s, d, t = lax.axis_index("section"), lax.axis_index("dp"), lax.axis_index("tensor")

    barrier = pltpu.get_barrier_semaphore()
    greeted = [(s, d + 1 - 2 * (d % 2), t), (1 - s, d, t)]
    greeted += [(s, (d + 2 * k) % 8, t) for k in range(1, 4)]
    greeted += [(s, d, (t + k) % 8) for k in range(1, 8)]
    for to in greeted:
        pl.semaphore_signal(barrier, inc=1, device_id=to, device_id_type=MESH)

    def fetch(src, dst, index):
        copy = pltpu.make_async_copy(src, dst, local_sems.at[index])
        copy.start()
        return copy

    def branch(section):
        first = section == 0
        links = Links(sems)
        hidden_group = Group(section, "dp" if first else "tensor", d, t)
        model_group = Group(section, "tensor" if first else "dp", d, t)
        width_index, unit_index = (d, t) if first else (t, d)
        features = pl.ds(pl.multiple_of(width_index * MODEL, MODEL), MODEL)
        units = pl.ds(pl.multiple_of(unit_index * UNITS, UNITS), UNITS)
        g, hg = model_group, hidden_group
        get_own = fetch(tokens if first else out_grad, raw, 0)
        weights = [(up.at[0], U, 1), (down.at[0], V, 2)]
        gets = {}
        for src, dst, index in weights if first else weights[::-1]:
            gets[index] = fetch(src, dst, index)
        small = [
            fetch(gain.at[:, features], gain_row, 3), fetch(shift.at[:, features], shift_row, 4),
            fetch(up_bias.at[:, units], up_row, 5), fetch(down_bias.at[:, features], down_row, 6),
        ]

        def need(index):
            if index in gets:
                gets.pop(index).wait()

        get_own.wait()
        own_rows = moved(halves_matrix(), raw[...]) if HALVES == 2 else raw[...]
        for h in range(HALVES):
            xall[0, h, g.hi, g.lo] = own_rows[h * BLOCK:(h + 1) * BLOCK]
        for copy in small:
            copy.wait()
        pl.semaphore_wait(barrier, len(greeted))

        def own_x(h):
            return xall[0, h, g.hi, g.lo].astype(F32)

        def scatter_of(group):
            return PairScatter if group.axis == "dp" else DirectScatter

        def gather_of(group):
            return PairGather if group.axis == "dp" else DirectGather

        def scatter_hidden(slot, h):
            return [
                scatter_of(hg)(links, hg, f"h{slot}{h}{c}", part.at[slot, h, c], from_pair.at[slot, h, c],
                               pair_sum.at[slot, h, c], received.at[slot, h, c])
                for c in range(N_CHUNKS)
            ]

        def scatter_model(slot, h):
            return [
                scatter_of(g)(links, g, f"m{slot}{h}{m}", part_m.at[slot, h, m], from_pair_m.at[slot, h, m],
                              pair_sum_m.at[slot, h, m], received_m.at[slot, h, m])
                for m in range(M_CHUNKS)
            ]

        def gather_hidden(slot, h):
            return [gather_of(hg)(links, hg, f"g{slot}{h}{c}", hall.at[slot, h, c], received.at[slot, h, c]) for c in range(N_CHUNKS)]

        def gather_rows(name, slot, h):
            return gather_of(g)(links, g, f"{name}{h}", xall.at[slot, h], received_m.at[slot, h, 0])

        def start_hidden(x_ref, w_ref, transposed, scatters):
            for c, scatter in enumerate(scatters):
                x = x_ref[...].reshape(HALF, MODEL)
                for at in range(0, N_WIDTH, 512):
                    value = product(x, w_ref, transposed, 0, MODEL, c * N_WIDTH + at, 512)
                    scatter.part[:, :, :, pl.ds(at, 512)] = value.astype(BF16).reshape(4, 2, BLOCK, 512)
                scatter.send()
                if c >= 1:
                    yield from scatters[c - 1].middle()
            yield from scatters[-1].middle()

        def to_model(h, gathers, w_ref, transposed, scatters):
            for c, gather in enumerate(gathers):
                yield
                gather.ready()
                x = gather.whole[...].reshape(HALF, N_WIDTH)
                if c < N_CHUNKS - 1:
                    for at in range(0, MODEL, 512):
                        value = product(x, w_ref, transposed, c * N_WIDTH, N_WIDTH, at, 512)
                        acc[h, :, pl.ds(at, 512)] = value if c == 0 else acc[h, :, pl.ds(at, 512)] + value
                    continue
                for m, scatter in enumerate(scatters):
                    for at in range(0, M_WIDTH, 512):
                        value = product(x, w_ref, transposed, c * N_WIDTH, N_WIDTH, m * M_WIDTH + at, 512)
                        if c > 0:
                            value = value + acc[h, :, pl.ds(m * M_WIDTH + at, 512)]
                        scatter.part[:, :, :, pl.ds(at, 512)] = value.astype(BF16).reshape(4, 2, BLOCK, 512)
                    scatter.send()
                    if m >= 1:
                        yield from scatters[m - 1].middle()
            yield from scatters[-1].middle()

        def through(h, scatters, gathers, epilogue, w_ref, transposed, scatters_out):
            for c, scatter in enumerate(scatters):
                yield
                value = epilogue(h, unit_slice(c), scatter.finish())
                gathers[c].whole[hg.hi, hg.lo] = value.astype(BF16)
                gathers[c].send()
                if c >= 1:
                    yield from gathers[c - 1].forward()
            yield from gathers[-1].forward()
            yield from to_model(h, gathers, w_ref, transposed, scatters_out)

        def finish_model(scatters):
            yield
            return jnp.concatenate([scatter.finish() for scatter in scatters], axis=1)

        def normalize_all(h, source):
            for hi in range(4):
                for lo in range(2):
                    average = stats[h, hi, lo][:, 0:1]
                    inverse_dev = stats[h, hi, lo][:, 64:65]
                    unit = (source[hi, lo].astype(F32) - average) * inverse_dev
                    xn[h, hi, lo] = (unit * gain_row[...] + shift_row[...]).astype(BF16)

        def swapped(h, source):
            rows = moved(swap_matrix(), source[...].reshape(HALF, MODEL))
            xn2[h] = rows.reshape(4, 2, BLOCK, MODEL)

        def unit_slice(c):
            return pl.ds(c * N_WIDTH, N_WIDTH)

        def input_gradient(h, incoming, norm_grad, rows):
            average, inverse_dev = own_stats[h][:, 0:1], own_stats[h][:, 64:65]
            unit = (rows - average) * inverse_dev
            scaled = norm_grad * gain_row[...]
            table = moments.at[h, 2]
            table[0] = two_lanes(jnp.sum(scaled, 1, keepdims=True), jnp.sum(scaled * unit, 1, keepdims=True))
            total = yield from (pairwise if first else exchange)(links, hg, f"sums{h}", table, add_all)
            first_mean, second_mean = total[:, 0:1] / D, total[:, 64:65] / D
            return (incoming + inverse_dev * (scaled - first_mean - unit * second_mean)).astype(BF16)

        def store_rows(ref, rows):
            rows = rows[...].reshape(ROWS, MODEL)
            ref[0] = moved(whole_matrix(), rows) if HALVES == 2 else rows

        partners = [(1, 2 * k + t % 2, d) for k in range(4)]

        def y0_cross(h):
            return Cross(links, g, f"y0{h}", xall.at[1, h], partners)

        def stats_cross(h):
            return Cross(links, g, f"y0stats{h}", stats.at[h], partners)

        def transposed_sems(h):
            return links.sem(f"g1{h}/send"), links.sem(f"g1{h}/recv")

        def first_chain(h):
            gather = gather_rows("x", 0, h)
            gather.send()
            moments[h, 0, 0] = local_moments(own_x(h))
            joined = yield from pairwise(links, hg, f"first{h}", moments.at[h, 0], join_moments)
            own_stats[h] = row_stats(joined)
            stats[h, g.hi, g.lo] = own_stats[h]
            stats_gather = DirectGather(links, g, f"st{h}", stats.at[h], moments.at[h, 0, pl.ds(0, 7)])
            stats_gather.send()
            yield
            gather.ready()
            stats_gather.ready()
            normalize_all(h, xall.at[0, h])
            need(1)
            scatters = scatter_hidden(0, h)
            yield from start_hidden(xn.at[h], U, False, scatters)
            need(2)

            def forward_hidden(h, at, value):
                value = value + up_row[:, at]
                pre[h, :, at] = value
                return gelu_value(value)

            scatters_out = scatter_model(0, h)
            yield from through(h, scatters, gather_hidden(0, h), forward_hidden, V, False, scatters_out)
            mixed = yield from finish_model(scatters_out)
            y0 = (own_x(h) + mixed + down_row[...]).astype(BF16)
            sendbuf[0, h] = y0
            y0_cross(h).send(sendbuf.at[0, h], sendbuf.at[pl.ds(0, 4), h])
            moments[h, 1, 0] = local_moments(y0.astype(F32))
            joined = yield from pairwise(links, hg, f"second{h}", moments.at[h, 1], join_moments)
            cross_stats[h, 0] = row_stats(joined)
            stats_cross(h).send(cross_stats.at[h, 0], cross_stats.at[h])
            if h == HALVES - 1:
                store_rows(out_ref, sendbuf.at[0])

            yield
            place = xall.at[1, h, g.hi, g.lo]
            links.wait_recv(place, transposed_sems(h)[1], g.pair())
            gather = gather_rows("g1x", 1, h)
            gather.send()
            yield
            gather.ready()
            swapped(h, xall.at[1, h])
            scatters = scatter_hidden(1, h)
            yield from start_hidden(xn2.at[h], V, True, scatters)

            def backward_hidden(h, at, value):
                return value * gelu_slope(pre[h, :, at])

            scatters_out = scatter_model(1, h)
            yield from through(h, scatters, gather_hidden(1, h), backward_hidden, U, True, scatters_out)
            norm_grad = yield from finish_model(scatters_out)
            incoming = xn2[h, g.hi, g.lo].astype(F32)
            gradbuf[h] = yield from input_gradient(h, incoming, norm_grad, own_x(h))
            if h == HALVES - 1:
                store_rows(grad_ref, gradbuf)

        def early_chain(h):
            gather = gather_rows("x", 0, h)
            gather.send()
            yield from gather.forward()
            yield
            gather.ready()
            need(2)
            scatters = scatter_hidden(0, h)
            yield from start_hidden(xall.at[0, h], V, True, scatters)
            for c in range(N_CHUNKS):
                yield
                hidden_grad[h, :, unit_slice(c)] = scatters[c].finish()

        def main_chain(h):
            rows, row_numbers = y0_cross(h), stats_cross(h)
            yield from rows.receive()
            yield from row_numbers.receive()
            yield
            rows.ready()
            row_numbers.ready()
            normalize_all(h, xall.at[1, h])
            swapped(h, xn.at[h])
            need(1)
            scatters = scatter_hidden(1, h)
            yield from start_hidden(xn2.at[h], U, False, scatters)
            pick = pick_matrix(d)
            y0_own[h] = jnp.dot(pick.astype(BF16), xall[1, h].reshape(HALF, MODEL), preferred_element_type=F32)
            own_stats[h] = jnp.dot(
                pick, stats[h].reshape(HALF, 128), preferred_element_type=F32, precision=lax.Precision.HIGHEST
            )

            def backward_hidden(h, at, value):
                value = value + up_row[:, at]
                pre[h, :, at] = value
                return hidden_grad[h, :, at] * gelu_slope(value)

            scatters_out = scatter_model(0, h)
            yield from through(h, scatters, gather_hidden(0, h), backward_hidden, U, True, scatters_out)
            norm_grad = yield from finish_model(scatters_out)
            gradbuf[h] = yield from input_gradient(h, own_x(h), norm_grad, y0_own[h])
            send_sem, recv_sem = transposed_sems(h)
            links.send(gradbuf.at[h], xall.at[1, h, g.hi, g.lo], (0, t, d), send_sem, recv_sem)
            links.later(gradbuf.at[h], send_sem, g.pair())

        def late_chain(h):
            gathers = gather_hidden(1, h)
            for c, gather in enumerate(gathers):
                gather.whole[hg.hi, hg.lo] = gelu_value(pre[h, :, unit_slice(c)]).astype(BF16)
                gather.send()
            scatters_out = scatter_model(1, h)
            yield from to_model(h, gathers, V, False, scatters_out)
            mixed = yield from finish_model(scatters_out)
            sendbuf[0, h] = (y0_own[h] + mixed + down_row[...]).astype(BF16)

        if first:
            drive([first_chain(h) for h in range(HALVES)])
        else:
            drive([early_chain(h) for h in range(HALVES)])
            links.finish()
            drive([main_chain(h) for h in range(HALVES)])
            store_rows(grad_ref, gradbuf)
            drive([late_chain(h) for h in range(HALVES)])
            store_rows(out_ref, sendbuf.at[0])
        links.finish()

    for section in range(2):
        pl.when(s == section)(functools.partial(branch, section))
    assert sum(width for _, width in SEM_NAMES.values()) <= SEM_COUNT


def shards(tokens, out_grad, norm_gain, norm_shift, up_weight, up_bias, down_weight, down_bias):
    vmem = pltpu.VMEM
    hidden, model = (2, HALVES, N_CHUNKS), (2, HALVES, M_CHUNKS)
    return pl.pallas_call(
        kernel,
        out_shape=[jax.ShapeDtypeStruct((1, ROWS, MODEL), BF16)] * 2,
        in_specs=[pl.BlockSpec(memory_space=pl.ANY)] * 8,
        out_specs=[pl.BlockSpec(memory_space=vmem)] * 2,
        scratch_shapes=[
            vmem((MODEL, UNITS), BF16),
            vmem((UNITS, MODEL), BF16),
            vmem((1, MODEL), F32),
            vmem((1, MODEL), F32),
            vmem((1, UNITS), F32),
            vmem((1, MODEL), F32),
            vmem((ROWS, MODEL), BF16),
            vmem((2, HALVES, 4, 2, BLOCK, MODEL), BF16),
            vmem((HALVES, 4, 2, BLOCK, MODEL), BF16),
            vmem((HALVES, 4, 2, BLOCK, MODEL), BF16),
            vmem(hidden + (4, 2, BLOCK, N_WIDTH), BF16),
            vmem(hidden + (4, BLOCK, N_WIDTH), BF16),
            vmem(hidden + (4, BLOCK, N_WIDTH), BF16),
            vmem(hidden + (7, BLOCK, N_WIDTH), BF16),
            vmem(hidden + (4, 2, BLOCK, N_WIDTH), BF16),
            vmem((HALVES, HALF, MODEL), F32),
            vmem(model + (4, 2, BLOCK, M_WIDTH), BF16),
            vmem(model + (4, BLOCK, M_WIDTH), BF16),
            vmem(model + (4, BLOCK, M_WIDTH), BF16),
            vmem(model + (7, BLOCK, M_WIDTH), BF16),
            vmem((HALVES, BLOCK, UNITS), F32),
            vmem((HALVES, BLOCK, UNITS), F32),
            vmem((HALVES, 3, 8, BLOCK, 128), F32),
            vmem((HALVES, 4, 2, BLOCK, 128), F32),
            vmem((HALVES, 4, BLOCK, 128), F32),
            vmem((4, HALVES, BLOCK, MODEL), BF16),
            vmem((HALVES, BLOCK, MODEL), BF16),
            vmem((HALVES, BLOCK, MODEL), F32),
            vmem((HALVES, BLOCK, 128), F32),
            pltpu.SemaphoreType.DMA((SEM_COUNT,)),
            pltpu.SemaphoreType.DMA((8,)),
        ],
        compiler_params=pltpu.CompilerParams(
            collective_id=0, has_side_effects=True, vmem_limit_bytes=58 * 2**20
        ),
        cost_estimate=pl.CostEstimate(flops=10**10, bytes_accessed=2 * 10**7, transcendentals=10**5),
        name="relay",
    )(tokens, out_grad, norm_gain, norm_shift, up_weight, up_bias, down_weight, down_bias)


def solution(mesh):
    placed = (
        P("tensor", "dp"),
        P("tensor", "dp"),
        P("section", None),
        P("section", None),
        P("section", "dp", "tensor"),
        P("section", None),
        P("section", "tensor", "dp"),
        P("section", None),
    )
    return jax.shard_map(
        shards,
        mesh=mesh,
        in_specs=placed,
        out_specs=(P("section", "tensor", "dp"), P("section", "tensor", "dp")),
        check_vma=False,
    )
```

time: 216 us -> 191 us (0.88)
  Pallas kernels: 212 us -> 187 us
    pallas_call x1, Pallas kernels: 212 us -> 187 us  [shards(): pl.pallas_call(kernel, out_shape=[jax.ShapeDtypeStruct((1, ROWS, MODEL),...]
where the time goes in v2:
time: 191 us
  Pallas kernels  187 us (98%)
  local copies, waits for them, and re-layouts  3.08 us (2%)
    pallas_call x1, Pallas kernels, shards(): pl.pallas_call(kernel, out_shape=[jax.ShapeDtypeStruct((1, ROWS, MODEL),...  187 us

profile of v2, /device:TPU:1, one launch (start us, length us, event | category | flops | bytes accessed | tf_op | source)
XLA Modules:
  0.0 190.5 jit_solution(15935855357765504110)
XLA Ops:
  0.6 186.8 %relay.1 = (bf16[1,32,1536]{2,1,0:T(8,128)(2,1)}, bf16[1,32,1536]{2,1,0:T(8,128)(2,1)}) custom-call(bf16[32,1536]{1,0:T(8,128)(2,1)} %tokens.1, bf16[32,1536]{1,0:T(8,128)(2,1)} %out_grad.1, f32[1,12288]{1,0:T(1,128)} %gain.1, f32[1,12288]{1,0:T(1,128)} %shift.1, bf16[1,1536,3072]{2,1,0:T(8,128)(2,1)} %up.1, f32[1,24576]{1,0:T(1,128)} %up_bias.1, ...), custom_call_target="tpu_custom_call" | custom-call | flops 10000000000 | bytes 20000000 | tf_op jit(solution)/shard_map/relay/pallas_call | solution.py:637
  187.5 1.5 copy.12
  189.0 1.5 copy.13

commit v3 on v2

--- a/solution.py
+++ b/solution.py
@@ -16,6 +16,7 @@
 HALF = 8 * BLOCK
 N_CHUNKS, N_WIDTH = 2, 1536
 M_CHUNKS, M_WIDTH = 1, 1536
+FORWARD_LEAD, MAIN_LEAD, BACKWARD_LEAD = 0, 2, 0
 FAR_FIRST = (4, 3, 5, 2, 6, 7, 1)
 MESH = pl.DeviceIdType.MESH
 F32, BF16 = jnp.float32, jnp.bfloat16
@@ -261,8 +262,13 @@
     return combine([table[k] for k in range(2, 6)])
 
 
-def drive(chains):
+def drive(chains, lead=0):
     alive = list(chains)
+    if lead:
+        for chain in alive:
+            next(chain)
+    for _ in range(lead):
+        next(alive[0])
     while alive:
         for chain in list(alive):
             try:
@@ -325,6 +331,16 @@
 
 def moved(matrix, rows):
     return jnp.dot(matrix, rows, preferred_element_type=F32).astype(BF16)
+
+
+def transpose_into(target, source):
+    rows, columns = source.shape
+
+    @pl.loop(0, rows // 512)
+    def _(i):
+        at = pl.ds(pl.multiple_of(i * 512, 512), 512)
+        for j in range(0, columns, 512):
+            target[pl.ds(j, 512), at] = source[at, pl.ds(j, 512)].T
 
 
 def product(x, w_ref, transposed, k0, depth, n0, width):
@@ -338,7 +354,7 @@
 
 def kernel(
     tokens, out_grad, gain, shift, up, up_bias, down, down_bias, out_ref, grad_ref,
-    U, V, gain_row, shift_row, up_row, down_row, raw, xall, xn, xn2, part, from_pair, pair_sum, received,
+    U, V, W, gain_row, shift_row, up_row, down_row, raw, xall, xn, xn2, part, from_pair, pair_sum, received,
     hall, acc, part_m, from_pair_m, pair_sum_m, received_m, pre, hidden_grad, moments, stats, cross_stats,
     sendbuf, gradbuf, y0_own, own_stats, sems, local_sems,
 ):
@@ -423,9 +439,7 @@
                     value = product(x, w_ref, transposed, 0, MODEL, c * N_WIDTH + at, 512)
                     scatter.part[:, :, :, pl.ds(at, 512)] = value.astype(BF16).reshape(4, 2, BLOCK, 512)
                 scatter.send()
-                if c >= 1:
-                    yield from scatters[c - 1].middle()
-            yield from scatters[-1].middle()
+                yield from scatter.middle()
 
         def to_model(h, gathers, w_ref, transposed, scatters):
             for c, gather in enumerate(gathers):
@@ -497,13 +511,13 @@
         def y0_cross(h):
             return Cross(links, g, f"y0{h}", xall.at[1, h], partners)
 
-        def stats_cross(h):
-            return Cross(links, g, f"y0stats{h}", stats.at[h], partners)
+        def stats_sems(h):
+            return links.sem(f"y0stats{h}/send"), links.sem(f"y0stats{h}/recv")
 
         def transposed_sems(h):
             return links.sem(f"g1{h}/send"), links.sem(f"g1{h}/recv")
 
-        def first_chain(h):
+        def forward_chain(h):
             gather = gather_rows("x", 0, h)
             gather.send()
             moments[h, 0, 0] = local_moments(own_x(h))
@@ -535,10 +549,12 @@
             moments[h, 1, 0] = local_moments(y0.astype(F32))
             joined = yield from pairwise(links, hg, f"second{h}", moments.at[h, 1], join_moments)
             cross_stats[h, 0] = row_stats(joined)
-            stats_cross(h).send(cross_stats.at[h, 0], cross_stats.at[h])
-            if h == HALVES - 1:
-                store_rows(out_ref, sendbuf.at[0])
-
+            send_sem, recv_sem = stats_sems(h)
+            for q in range(8):
+                links.send(cross_stats.at[h, 0], stats.at[h, g.hi, g.lo], (1, q, d), send_sem, recv_sem)
+            links.later(cross_stats.at[h], send_sem, g.pair())
+
+        def backward_chain(h):
             yield
             place = xall.at[1, h, g.hi, g.lo]
             links.wait_recv(place, transposed_sems(h)[1], g.pair())
@@ -548,18 +564,16 @@
             gather.ready()
             swapped(h, xall.at[1, h])
             scatters = scatter_hidden(1, h)
-            yield from start_hidden(xn2.at[h], V, True, scatters)
+            yield from start_hidden(xn2.at[h], U, False, scatters)
 
             def backward_hidden(h, at, value):
                 return value * gelu_slope(pre[h, :, at])
 
             scatters_out = scatter_model(1, h)
-            yield from through(h, scatters, gather_hidden(1, h), backward_hidden, U, True, scatters_out)
+            yield from through(h, scatters, gather_hidden(1, h), backward_hidden, W, False, scatters_out)
             norm_grad = yield from finish_model(scatters_out)
             incoming = xn2[h, g.hi, g.lo].astype(F32)
             gradbuf[h] = yield from input_gradient(h, incoming, norm_grad, own_x(h))
-            if h == HALVES - 1:
-                store_rows(grad_ref, gradbuf)
 
         def early_chain(h):
             gather = gather_rows("x", 0, h)
@@ -575,12 +589,11 @@
                 hidden_grad[h, :, unit_slice(c)] = scatters[c].finish()
 
         def main_chain(h):
-            rows, row_numbers = y0_cross(h), stats_cross(h)
+            rows = y0_cross(h)
             yield from rows.receive()
-            yield from row_numbers.receive()
             yield
             rows.ready()
-            row_numbers.ready()
+            links.wait_recv(stats.at[h], stats_sems(h)[1], g.pair())
             normalize_all(h, xall.at[1, h])
             swapped(h, xn.at[h])
             need(1)
@@ -598,7 +611,7 @@
                 return hidden_grad[h, :, at] * gelu_slope(value)
 
             scatters_out = scatter_model(0, h)
-            yield from through(h, scatters, gather_hidden(0, h), backward_hidden, U, True, scatters_out)
+            yield from through(h, scatters, gather_hidden(0, h), backward_hidden, W, False, scatters_out)
             norm_grad = yield from finish_model(scatters_out)
             gradbuf[h] = yield from input_gradient(h, own_x(h), norm_grad, y0_own[h])
             send_sem, recv_sem = transposed_sems(h)
@@ -616,11 +629,18 @@
             sendbuf[0, h] = (y0_own[h] + mixed + down_row[...]).astype(BF16)
 
         if first:
-            drive([first_chain(h) for h in range(HALVES)])
+            drive([forward_chain(h) for h in range(HALVES)], FORWARD_LEAD)
+            store_rows(out_ref, sendbuf.at[0])
+            transpose_into(W, U)
+            transpose_into(U, V)
+            drive([backward_chain(h) for h in range(HALVES)], BACKWARD_LEAD)
+            store_rows(grad_ref, gradbuf)
         else:
             drive([early_chain(h) for h in range(HALVES)])
             links.finish()
-            drive([main_chain(h) for h in range(HALVES)])
+            need(1)
+            transpose_into(W, U)
+            drive([main_chain(h) for h in range(HALVES)], MAIN_LEAD)
             store_rows(grad_ref, gradbuf)
             drive([late_chain(h) for h in range(HALVES)])
             store_rows(out_ref, sendbuf.at[0])
@@ -631,16 +651,22 @@
     assert sum(width for _, width in SEM_NAMES.values()) <= SEM_COUNT
 
 
+def hand_over(out, grad, out_ref, grad_ref):
+    out_ref[...] = out[...]
+    grad_ref[...] = grad[...]
+
+
 def shards(tokens, out_grad, norm_gain, norm_shift, up_weight, up_bias, down_weight, down_bias):
     vmem = pltpu.VMEM
     hidden, model = (2, HALVES, N_CHUNKS), (2, HALVES, M_CHUNKS)
-    return pl.pallas_call(
+    results = pl.pallas_call(
         kernel,
         out_shape=[jax.ShapeDtypeStruct((1, ROWS, MODEL), BF16)] * 2,
         in_specs=[pl.BlockSpec(memory_space=pl.ANY)] * 8,
         out_specs=[pl.BlockSpec(memory_space=vmem)] * 2,
         scratch_shapes=[
             vmem((MODEL, UNITS), BF16),
+            vmem((UNITS, MODEL), BF16),
             vmem((UNITS, MODEL), BF16),
             vmem((1, MODEL), F32),
             vmem((1, MODEL), F32),
@@ -664,7 +690,7 @@
             vmem((HALVES, BLOCK, UNITS), F32),
             vmem((HALVES, 3, 8, BLOCK, 128), F32),
             vmem((HALVES, 4, 2, BLOCK, 128), F32),
-            vmem((HALVES, 4, BLOCK, 128), F32),
+            vmem((HALVES, 8, BLOCK, 128), F32),
             vmem((4, HALVES, BLOCK, MODEL), BF16),
             vmem((HALVES, BLOCK, MODEL), BF16),
             vmem((HALVES, BLOCK, MODEL), F32),
@@ -678,6 +704,13 @@
         cost_estimate=pl.CostEstimate(flops=10**10, bytes_accessed=2 * 10**7, transcendentals=10**5),
         name="relay",
     )(tokens, out_grad, norm_gain, norm_shift, up_weight, up_bias, down_weight, down_bias)
+    return pl.pallas_call(
+        hand_over,
+        out_shape=[jax.ShapeDtypeStruct((1, ROWS, MODEL), BF16)] * 2,
+        in_specs=[pl.BlockSpec(memory_space=vmem)] * 2,
+        out_specs=[pl.BlockSpec(memory_space=vmem)] * 2,
+        name="hand_over",
+    )(*results)
 
 
 def solution(mesh):

time: 191 us -> 182 us (0.953)
  Pallas kernels: 187 us -> 181 us
  local copies, waits for them, and re-layouts: 3.08 us -> 0 us
    pallas_call x1, Pallas kernels: 187 us -> 180 us  [shards(): pl.pallas_call(kernel, out_shape=[jax.ShapeDtypeStruct((1, ROWS, MODEL),...]
    unnamed x2 -> x0, local copies, waits for them, and re-layouts: 3.08 us -> none
where the time goes in v3:
time: 182 us
  Pallas kernels  181 us (99%)
    pallas_call x1, Pallas kernels, shards(): pl.pallas_call(kernel, out_shape=[jax.ShapeDtypeStruct((1, ROWS, MODEL),...  180 us

profile of v3, /device:TPU:1, one launch (start us, length us, event | category | flops | bytes accessed | tf_op | source)
XLA Modules:
  0.0 181.9 jit_solution(14501402961956793894)
XLA Ops:
  0.6 179.6 %relay.1 = (bf16[1,32,1536]{2,1,0:T(8,128)(2,1)}, bf16[1,32,1536]{2,1,0:T(8,128)(2,1)}) custom-call(bf16[32,1536]{1,0:T(8,128)(2,1)} %tokens.1, bf16[32,1536]{1,0:T(8,128)(2,1)} %out_grad.1, f32[1,12288]{1,0:T(1,128)} %gain.1, f32[1,12288]{1,0:T(1,128)} %shift.1, bf16[1,1536,3072]{2,1,0:T(8,128)(2,1)} %up.1, f32[1,24576]{1,0:T(1,128)} %up_bias.1, ...), custom_call_target="tpu_custom_call" | custom-call | flops 10000000000 | bytes 20000000 | tf_op jit(solution)/shard_map/relay/pallas_call | solution.py:662
  180.3 1.6 hand_over.1

commit v4 on v3

--- a/solution.py
+++ b/solution.py
@@ -16,8 +16,8 @@
 HALF = 8 * BLOCK
 N_CHUNKS, N_WIDTH = 2, 1536
 M_CHUNKS, M_WIDTH = 1, 1536
-FORWARD_LEAD, MAIN_LEAD, BACKWARD_LEAD = 0, 2, 0
-FAR_FIRST = (4, 3, 5, 2, 6, 7, 1)
+FORWARD_LEAD, MAIN_LEAD, BACKWARD_LEAD = 0, 1, 0
+SEND_ORDER = (1, 7, 3, 5, 4, 2, 6)
 MESH = pl.DeviceIdType.MESH
 F32, BF16 = jnp.float32, jnp.bfloat16
 
@@ -143,7 +143,7 @@
     def send(self):
         g, k = self.group, self.links
         send_sem = k.sem(f"{self.name}/send")
-        for step in FAR_FIRST:
+        for step in SEND_ORDER:
             to = (g.index + step) % 8
             k.send(self.part.at[to // 2, to % 2], self.received.at[step - 1], g.member(to), send_sem,
                    k.sem(f"{self.name}/recv"))
@@ -198,7 +198,7 @@
         g, k = self.group, self.links
         own = self.whole.at[g.hi, g.lo]
         send_sem = k.sem(f"{self.name}/send")
-        for step in FAR_FIRST:
+        for step in SEND_ORDER:
             k.send(own, own, g.member((g.index + step) % 8), send_sem, k.sem(f"{self.name}/recv"))
         k.later(self.seven, send_sem, g.pair())
 
@@ -238,7 +238,7 @@
 
 def exchange(links, group, name, table, combine):
     send_sem, recv_sem = links.sem(f"{name}/send"), links.sem(f"{name}/recv")
-    for step in FAR_FIRST:
+    for step in SEND_ORDER:
         links.send(table.at[0], table.at[step], group.member((group.index + step) % 8), send_sem, recv_sem)
     links.later(table.at[pl.ds(1, 7)], send_sem, group.pair())
     yield
@@ -399,12 +399,15 @@
         own_rows = moved(halves_matrix(), raw[...]) if HALVES == 2 else raw[...]
         for h in range(HALVES):
             xall[0, h, g.hi, g.lo] = own_rows[h * BLOCK:(h + 1) * BLOCK]
+        def own_x(h):
+            return xall[0, h, g.hi, g.lo].astype(F32)
+
+        if first:
+            for h in range(HALVES):
+                moments[h, 0, 0] = local_moments(own_x(h))
         for copy in small:
             copy.wait()
         pl.semaphore_wait(barrier, len(greeted))
-
-        def own_x(h):
-            return xall[0, h, g.hi, g.lo].astype(F32)
 
         def scatter_of(group):
             return PairScatter if group.axis == "dp" else DirectScatter
@@ -520,7 +523,6 @@
         def forward_chain(h):
             gather = gather_rows("x", 0, h)
             gather.send()
-            moments[h, 0, 0] = local_moments(own_x(h))
             joined = yield from pairwise(links, hg, f"first{h}", moments.at[h, 0], join_moments)
             own_stats[h] = row_stats(joined)
             stats[h, g.hi, g.lo] = own_stats[h]
@@ -633,6 +635,7 @@
             store_rows(out_ref, sendbuf.at[0])
             transpose_into(W, U)
             transpose_into(U, V)
+            links.finish()
             drive([backward_chain(h) for h in range(HALVES)], BACKWARD_LEAD)
             store_rows(grad_ref, gradbuf)
         else:

time: 182 us -> 178 us (0.978)
  Pallas kernels: 181 us -> 177 us
    pallas_call x1, Pallas kernels: 180 us -> 176 us  [shards(): pl.pallas_call(kernel, out_shape=[jax.ShapeDtypeStruct((1, ROWS, MODEL),...]
where the time goes in v4:
time: 178 us
  Pallas kernels  177 us (99%)
    pallas_call x1, Pallas kernels, shards(): pl.pallas_call(kernel, out_shape=[jax.ShapeDtypeStruct((1, ROWS, MODEL),...  176 us

profile of v4, /device:TPU:1, one launch (start us, length us, event | category | flops | bytes accessed | tf_op | source)
XLA Modules:
  0.0 178.0 jit_solution(1643945070045188547)
XLA Ops:
  0.6 175.7 %relay.1 = (bf16[1,32,1536]{2,1,0:T(8,128)(2,1)}, bf16[1,32,1536]{2,1,0:T(8,128)(2,1)}) custom-call(bf16[32,1536]{1,0:T(8,128)(2,1)} %tokens.1, bf16[32,1536]{1,0:T(8,128)(2,1)} %out_grad.1, f32[1,12288]{1,0:T(1,128)} %gain.1, f32[1,12288]{1,0:T(1,128)} %shift.1, bf16[1,1536,3072]{2,1,0:T(8,128)(2,1)} %up.1, f32[1,24576]{1,0:T(1,128)} %up_bias.1, ...), custom_call_target="tpu_custom_call" | custom-call | flops 10000000000 | bytes 20000000 | tf_op jit(solution)/shard_map/relay/pallas_call | solution.py:665
  176.3 1.6 hand_over.1

commit v5 on v4

--- a/solution.py
+++ b/solution.py
@@ -612,8 +612,11 @@
                 pre[h, :, at] = value
                 return hidden_grad[h, :, at] * gelu_slope(value)
 
+            gathers = [
+                PairGather(links, hg, f"g0{h}{c}", hall.at[0, h, c], None) for c in range(N_CHUNKS)
+            ]
             scatters_out = scatter_model(0, h)
-            yield from through(h, scatters, gather_hidden(0, h), backward_hidden, W, False, scatters_out)
+            yield from through(h, scatters, gathers, backward_hidden, W, False, scatters_out)
             norm_grad = yield from finish_model(scatters_out)
             gradbuf[h] = yield from input_gradient(h, own_x(h), norm_grad, y0_own[h])
             send_sem, recv_sem = transposed_sems(h)

time: 178 us -> 178 us (level)
  no operation moved by 1% of the time
where the time goes in v5:
time: 178 us
  Pallas kernels  177 us (99%)
    pallas_call x1, Pallas kernels, shards(): pl.pallas_call(kernel, out_shape=[jax.ShapeDtypeStruct((1, ROWS, MODEL),...  175 us

profile of v5, /device:TPU:1, one launch (start us, length us, event | category | flops | bytes accessed | tf_op | source)
XLA Modules:
  0.0 177.6 jit_solution(5931539063983387064)
XLA Ops:
  0.6 175.3 %relay.1 = (bf16[1,32,1536]{2,1,0:T(8,128)(2,1)}, bf16[1,32,1536]{2,1,0:T(8,128)(2,1)}) custom-call(bf16[32,1536]{1,0:T(8,128)(2,1)} %tokens.1, bf16[32,1536]{1,0:T(8,128)(2,1)} %out_grad.1, f32[1,12288]{1,0:T(1,128)} %gain.1, f32[1,12288]{1,0:T(1,128)} %shift.1, bf16[1,1536,3072]{2,1,0:T(8,128)(2,1)} %up.1, f32[1,24576]{1,0:T(1,128)} %up_bias.1, ...), custom_call_target="tpu_custom_call" | custom-call | flops 10000000000 | bytes 20000000 | tf_op jit(solution)/shard_map/relay/pallas_call | solution.py:668
  176.0 1.6 hand_over.1
